TPU v7x, 512 devices: a whole 4x8x8 slice. The times are simulated.
512 devices in a mesh: src: 32 (over x, z), tgt: 16 (over y, core).
Axes of the slice: x: 4, y: 8, z: 8, core: 2. Of those that a mesh axis runs over, the one named last changes fastest.
Arguments:
- source_points: bfloat16 [16, 65536], P(None, 'src'), may hold values from -8 to 8
- target_points: bfloat16 [16, 32768], P(None, 'tgt'), may hold values from -8 to 8
- source_logw: float32 [65536], P('src'), may hold values from -1 to 1
- target_logw: float32 [32768], P('tgt'), may hold values from -1 to 1
Outputs:
- pot_src: float32 [65536], P('src')
- pot_tgt: float32 [32768], P('tgt')
- row_ratio: float32 [65536], P('src')
- projected: float32 [16, 65536], P(None, 'src')
- pulled: float32 [16, 32768], P(None, 'tgt')
All inputs are finite; a program needn't handle non-finite values.
Results may differ from a plain program's by a relative error of at most 0.00089.
Values sent between devices are 32-bit elements; how exact they have to be, the bound alone decides.
No kernel may reach another device: no remote copies, remote signals or barrier semaphores. Data moves between devices by JAX's collectives and lax.ppermute only.
A program may use at most 64 MiB of HBM per device.

v0:
```python
import math

import jax
import jax.numpy as jnp
from jax import lax
from jax.sharding import PartitionSpec as P

ITERS = 2


epsilon = 0.1
far_below = -1e30


def per_device(source_points, target_points, source_logw, target_logw):
    features, row_count = source_points.shape
    col_count = target_points.shape[1]
    row_block = 256
    block_count = row_count // row_block
    src_parts = source_points.reshape(features, block_count, row_block).transpose(1, 0, 2)
    src_norms = jnp.sum(jnp.square(source_points.astype(jnp.float32)), axis=0).reshape(
        block_count, row_block
    )
    tgt_norms = jnp.sum(jnp.square(target_points.astype(jnp.float32)), axis=0)
    log_a = source_logw - math.log(row_count * lax.axis_size("src"))
    log_b = target_logw - math.log(col_count * lax.axis_size("tgt"))

    def cost_block(src_part, src_norm):
        inner_prod = lax.dot_general(
            src_part, target_points, (((0,), (0,)), ((), ())), preferred_element_type=jnp.float32
        )
        return (src_norm[:, None] + tgt_norms[None, :] - 2.0 * inner_prod) / features

    def row_update(pot_tgt):

        def row_advance(running, inputs):
            scores = (pot_tgt[None, :] - cost_block(inputs[0], inputs[1])) / epsilon
            peaks = jnp.max(scores, axis=1)
            totals = jnp.sum(jnp.exp(scores - peaks[:, None]), axis=1)
            return (running, (peaks, totals))

        _, (peaks, totals) = lax.scan(
            row_advance, jnp.zeros((), jnp.float32), (src_parts, src_norms)
        )
        peaks = peaks.reshape(row_count)
        totals = totals.reshape(row_count)
        maximum = lax.pmax(peaks, "tgt")
        summed = lax.psum(totals * jnp.exp(peaks - maximum), "tgt")
        return epsilon * log_a - epsilon * (maximum + jnp.log(summed))

    def col_update(pot_src):
        pot_blocks = pot_src.reshape(block_count, row_block)

        def col_advance(running, inputs):
            scores = (inputs[2][:, None] - cost_block(inputs[0], inputs[1])) / epsilon
            peaks = jnp.maximum(running[0], jnp.max(scores, axis=0))
            totals = running[1] * jnp.exp(running[0] - peaks) + jnp.sum(
                jnp.exp(scores - peaks[None, :]), axis=0
            )
            return ((peaks, totals), None)

        start = (
            jnp.full((col_count,), far_below, jnp.float32),
            jnp.zeros((col_count,), jnp.float32),
        )
        (peaks, totals), _ = lax.scan(col_advance, start, (src_parts, src_norms, pot_blocks))
        maximum = lax.pmax(peaks, "src")
        summed = lax.psum(totals * jnp.exp(peaks - maximum), "src")
        return epsilon * log_b - epsilon * (maximum + jnp.log(summed))

    pot_tgt = jnp.zeros((col_count,), jnp.float32)
    pot_src = jnp.zeros((row_count,), jnp.float32)
    for sweep in range(ITERS):
        pot_src = row_update(pot_tgt)
        pot_tgt = col_update(pot_src)
    pot_blocks = pot_src.reshape(block_count, row_block)

    def collect(running, inputs):
        coupling = jnp.exp(
            (inputs[2][:, None] + pot_tgt[None, :] - cost_block(inputs[0], inputs[1])) / epsilon
        )
        row_mass = jnp.sum(coupling, axis=1)
        rounded = coupling.astype(jnp.bfloat16)
        row_sums = lax.dot_general(
            target_points, rounded, (((1,), (1,)), ((), ())), preferred_element_type=jnp.float32
        )
        col_sums = running[0] + lax.dot_general(
            inputs[0], rounded, (((1,), (0,)), ((), ())), preferred_element_type=jnp.float32
        )
        col_mass = running[1] + jnp.sum(coupling, axis=0)
        return ((col_sums, col_mass), (row_sums, row_mass))

    start = (jnp.zeros((features, col_count), jnp.float32), jnp.zeros((col_count,), jnp.float32))
    (col_sums, col_mass), (row_sums, row_mass) = lax.scan(
        collect, start, (src_parts, src_norms, pot_blocks)
    )
    row_sums = row_sums.transpose(1, 0, 2).reshape(features, row_count)
    row_mass = row_mass.reshape(row_count)
    row_total, mass_total = lax.psum((row_sums, row_mass), "tgt")
    projected = row_total / mass_total[None, :]
    row_ratio = mass_total * jnp.exp(-log_a) - 1.0
    col_total, cmass_total = lax.psum((col_sums, col_mass), "src")
    pulled = col_total / cmass_total[None, :]
    return (pot_src, pot_tgt, row_ratio, projected, pulled)


def solution(mesh):
    in_specs = (P(None, "src"), P(None, "tgt"), P("src"), P("tgt"))
    out_specs = (P("src"), P("tgt"), P("src"), P(None, "src"), P(None, "tgt"))
    return jax.shard_map(
        per_device, mesh=mesh, in_specs=in_specs, out_specs=out_specs, check_vma=False
    )
```

profile of v0, /device:TPU:1, one launch (start us, length us, event | category | flops | bytes accessed | tf_op | source)
XLA Modules:
  0.0 760.7 jit_solution(17412533144848478666)
XLA Ops:
  10.0 17.2 %while.67 = (s32[]{:T(128)}, f32[8,256]{1,0:T(8,128)S(1)}, f32[8,256]{1,0:T(8,128)S(1)}, f32[8,256]{1,0:T(8,128)S(1)}, f32[2048]{0:T(1024)S(1)}, /*index=5*/bf16...) while((s32[]{:T(128)}, f32[8,256]{1,0:T(8,128)S(1)}, f32[8,256]{1,0:T(8,128)S(1)}, ...), condition=%wide.region_5.6_spmd, body=%wide.region_2.5_spmd.sunk | while | flops 21495296 | bytes 4286573 | solution.py:42
  10.0 1.6 fusion.75
  12.1 1.6 fusion.75
  14.3 1.6 fusion.75
  16.4 1.6 fusion.75
  18.6 1.6 fusion.75
  20.7 1.6 fusion.75
  22.9 1.6 fusion.75
  25.0 1.6 fusion.75
  27.1 30.2 %pmax.28 = f32[2048]{0:T(1024)S(1)} all-reduce(f32[2048]{0:T(1024)S(1)} %bitcast.135), channel_id=1, replica_groups=mesh['src'=32,'tgt'=16] {'tgt'}, use_global_device_ids=true, to_apply=%region_6.7 | all-reduce | flops 2048 | bytes 16384 | tf_op jit(solution)/shard_map/pmax | solution.py:47
  57.4 24.1 %psum.56 = f32[2048]{0:T(1024)S(1)} all-reduce(f32[2048]{0:T(1024)S(1)} %exponential_multiply_fusion.3), channel_id=1, replica_groups=mesh['src'=32,'tgt'=16] {'tgt'}, use_global_device_ids=true, to_apply=%region_7.8 | all-reduce | flops 2048 | bytes 16384 | tf_op jit(solution)/shard_map/psum | solution.py:48
  81.5 15.4 %while.69 = (s32[]{:T(128)}, f32[2048]{0:T(1024)S(1)}, f32[2048]{0:T(1024)S(1)}, f32[8,256]{1,0:T(8,128)S(1)}, f32[8,256]{1,0:T(8,128)S(1)}, /*index=5*/f32[2048...) while((s32[]{:T(128)}, f32[2048]{0:T(1024)S(1)}, ...), condition=%wide.region_11.12_spmd.clone, body=%wide.region_8.11_spmd.clone.sunk | while | flops 21506048 | bytes 4388984 | solution.py:66
  81.6 1.5 fusion.79
  89.3 1.5 fusion.79
  93.1 1.5 fusion.79
  96.9 65.5 %pmax.29 = f32[2048]{0:T(1024)S(1)} all-reduce(f32[2048]{0:T(1024)S(1)} %get-tuple-element.234), channel_id=1, replica_groups=mesh['src'=32,'tgt'=16] {'src'}, use_global_device_ids=true, to_apply=%region_12.13 | all-reduce | flops 2048 | bytes 16384 | tf_op jit(solution)/shard_map/pmax | solution.py:67
  162.4 56.7 %psum.57 = f32[2048]{0:T(1024)S(1)} all-reduce(f32[2048]{0:T(1024)S(1)} %exponential_multiply_fusion.2), channel_id=1, replica_groups=mesh['src'=32,'tgt'=16] {'src'}, use_global_device_ids=true, to_apply=%region_13.14 | all-reduce | flops 2048 | bytes 16384 | tf_op jit(solution)/shard_map/psum | solution.py:68
  219.2 17.2 %while.68 = (s32[]{:T(128)}, f32[8,256]{1,0:T(8,128)S(1)}, f32[8,256]{1,0:T(8,128)S(1)}, f32[2048]{0:T(1024)S(1)}, f32[8,256]{1,0:T(8,128)S(1)}, /*index=5*/f32[...) while((s32[]{:T(128)}, f32[8,256]{1,0:T(8,128)S(1)}, ...), condition=%wide.region_17.18_spmd, body=%wide.region_14.17_spmd.sunk | while | flops 21495296 | bytes 4294773 | solution.py:42
  219.3 1.6 fusion.77
  221.4 1.6 fusion.77
  223.6 1.6 fusion.77
  225.7 1.6 fusion.77
  227.9 1.6 fusion.77
  230.0 1.6 fusion.77
  232.2 1.6 fusion.77
  234.4 1.6 fusion.77
  236.5 51.9 %pmax.30 = f32[2048]{0:T(1024)S(1)} all-reduce(f32[2048]{0:T(1024)S(1)} %bitcast.137), channel_id=1, replica_groups=mesh['src'=32,'tgt'=16] {'tgt'}, use_global_device_ids=true, to_apply=%region_18.19 | all-reduce | flops 2048 | bytes 16384 | tf_op jit(solution)/shard_map/pmax | solution.py:47
  288.4 24.1 %psum.58 = f32[2048]{0:T(1024)S(1)} all-reduce(f32[2048]{0:T(1024)S(1)} %exponential_multiply_fusion.1), channel_id=1, replica_groups=mesh['src'=32,'tgt'=16] {'tgt'}, use_global_device_ids=true, to_apply=%region_19.20 | all-reduce | flops 2048 | bytes 16384 | tf_op jit(solution)/shard_map/psum | solution.py:48
  313.1 15.4 %while.70 = (s32[]{:T(128)}, f32[2048]{0:T(1024)S(1)}, f32[2048]{0:T(1024)S(1)}, f32[8,256]{1,0:T(8,128)S(1)}, f32[8,256]{1,0:T(8,128)S(1)}, /*index=5*/f32[2048...) while((s32[]{:T(128)}, f32[2048]{0:T(1024)S(1)}, ...), condition=%wide.region_23.24_spmd.clone, body=%wide.region_20.23_spmd.clone.sunk | while | flops 21506048 | bytes 4388984 | solution.py:66
  316.9 1.5 fusion.82
  320.8 1.5 fusion.82
  328.4 59.1 %pmax.31 = f32[2048]{0:T(1024)S(1)} all-reduce(f32[2048]{0:T(1024)S(1)} %get-tuple-element.238), channel_id=1, replica_groups=mesh['src'=32,'tgt'=16] {'src'}, use_global_device_ids=true, to_apply=%region_24.25 | all-reduce | flops 2048 | bytes 16384 | tf_op jit(solution)/shard_map/pmax | solution.py:67
  387.6 57.2 %psum.59 = f32[2048]{0:T(1024)S(1)} all-reduce(f32[2048]{0:T(1024)S(1)} %exponential_multiply_fusion), channel_id=1, replica_groups=mesh['src'=32,'tgt'=16] {'src'}, use_global_device_ids=true, to_apply=%region_25.26 | all-reduce | flops 2048 | bytes 16384 | tf_op jit(solution)/shard_map/psum | solution.py:68
  444.8 21.6 %while.71 = (s32[]{:T(128)}, f32[16,2048]{1,0:T(8,128)S(1)}, f32[2048]{0:T(1024)S(1)}, f32[8,16,256]{2,1,0:T(8,128)S(1)}, f32[8,256]{1,0:T(8,128)S(1)}, /*index=...) while((s32[]{:T(128)}, f32[16,2048]{1,0:T(8,128)S(1)}, ...), condition=%wide.region_29.30_spmd.clone, body=%wide.region_26.29_spmd.clone.sunk | while | flops 55641856 | bytes 3892408 | solution.py:94
  444.8 2.0 fusion.89
  447.5 2.0 fusion.89
  450.2 2.0 fusion.89
  452.9 2.0 fusion.89
  455.6 2.0 fusion.89
  458.3 2.0 fusion.89
  461.0 2.0 fusion.89
  463.7 2.0 fusion.89
  467.9 57.8 %psum.63 = f32[2048]{0:T(1024)S(1)} all-reduce(f32[2048]{0:T(1024)S(1)} %get-tuple-element.243), channel_id=1, replica_groups=mesh['src'=32,'tgt'=16] {'src'}, use_global_device_ids=true, to_apply=%region_33.34 | all-reduce | flops 2048 | bytes 16384 | tf_op jit(solution)/shard_map/psum | solution.py:102
  525.7 66.1 %psum.60 = f32[2048]{0:T(1024)S(1)} all-reduce(f32[2048]{0:T(1024)S(1)} %bitcast.144), channel_id=1, replica_groups=mesh['src'=32,'tgt'=16] {'tgt'}, use_global_device_ids=true, to_apply=%region_30.31 | all-reduce | flops 2048 | bytes 16384 | tf_op jit(solution)/shard_map/psum | solution.py:99
  592.4 7.2 all-reduce.3.cloned.1.call-done
  599.6 1.6 broadcast_divide_fusion.1
  601.2 151.1 %all-reduce.5.cloned.1.call-done = f32[16,2048]{1,0:T(8,128)} async-done(((f32[16,2048]{1,0:T(8,128)}), f32[16,2048]{1,0:T(8,128)}) %all-reduce.5.cloned.1.call-update) | async-done | bytes 131088 | tf_op jit(solution)/shard_map/psum | solution.py:102
  752.3 1.6 broadcast_divide_fusion
  (259 shorter events, 41.7 us)
Async XLA Ops:
  7.2 592.5 %all-reduce.3.cloned.1.call-start = ((), (), s32[]{:S(2)}) async-start(), calls=%async_computation | async-start | bytes 262144 | tf_op jit(solution)/shard_map/psum | solution.py:99
  9.9 71.6 %copy-start.2 = (f32[2048]{0:T(1024)S(1)}, f32[2048]{0:T(1024)}, u32[]{:S(2)}) copy-start(f32[2048]{0:T(1024)} %param.16) | copy-start | bytes 24580
  81.5 137.7 %copy-start.4 = (f32[2048]{0:T(1024)S(1)}, f32[2048]{0:T(1024)}, u32[]{:S(2)}) copy-start(f32[2048]{0:T(1024)} %param.17) | copy-start | bytes 24580
  312.5 0.6 copy-start.3
  444.8 2.2 copy-start.1
  447.5 2.2 copy-start.1
  450.2 2.2 copy-start.1
  452.9 2.2 copy-start.1
  455.6 2.2 copy-start.1
  458.3 2.2 copy-start.1
  461.0 2.2 copy-start.1
  463.7 2.2 copy-start.1
  466.4 0.8 copy-start
  466.4 287.5 %copy-start.5 = (f32[2048]{0:T(1024)}, f32[2048]{0:T(1024)S(1)}, u32[]{:S(2)}) copy-start(f32[2048]{0:T(1024)S(1)} %get-tuple-element.952) | copy-start | bytes 24580
  467.1 285.2 %all-reduce.5.cloned.1.call-start = ((), (), s32[]{:S(2)}) async-start(), calls=%async_computation.1 | async-start | bytes 262144 | tf_op jit(solution)/shard_map/psum | solution.py:102
Sparse Core Ops, SparseCore 0:
  467.2 132.3 all-reduce.2
  603.5 148.7 all-reduce.4
where the time goes:
time: 766 us; the launch traced here: 761 us
  blocking collectives  493 us (64%)
  waiting for transfers between devices  159 us (21%)
  matrix products  70.7 us (9%)
  other arithmetic  17.9 us (2%)
  between operations  14.5 us (2%)
    psum x1, waiting for transfers between devices, per_device(): col_total, cmass_total = lax.psum((col_sums, col_mass), 'src')  151 us
    pmax x2, blocking collectives, col_update(): maximum = lax.pmax(peaks, 'src')  125 us
    psum x2, blocking collectives, col_update(): summed = lax.psum(totals * jnp.exp(peaks - maximum), 'src')  114 us
    pmax x2, blocking collectives, row_update(): maximum = lax.pmax(peaks, 'tgt')  82.1 us
    psum x1, blocking collectives, per_device(): row_total, mass_total = lax.psum((row_sums, row_mass), 'tgt')  66.1 us
    dot_general x40, matrix products, cost_block(): lax.dot_general(src_part, target_points, (((0,), (0,)), ((), ())), prefer...  65.7 us
    psum x1, blocking collectives, per_device(): col_total, cmass_total = lax.psum((col_sums, col_mass), 'src')  57.8 us
    psum x2, blocking collectives, row_update(): summed = lax.psum(totals * jnp.exp(peaks - maximum), 'tgt')  48.1 us
  transfers between devices with their start and end apart: 2, of which 2 were waited for; matrix products, arithmetic and copies ran while one was open for 0% of the time, Pallas kernels for 0%

commit v1 on v0

v1 whole, which is shorter than its diff:
```python
import math

import jax
import jax.numpy as jnp
from jax import lax
from jax.experimental import pallas as pl
from jax.experimental.pallas import tpu as pltpu
from jax.sharding import PartitionSpec as P

EPSILON = 0.1
LOG2E = math.log2(math.e)
KAPPA = LOG2E / EPSILON
LANES = 128
GROUP = 256
CHUNK = 256
DEPTH = 64
HALF = 8


def pieces(value):
    high = value.astype(jnp.bfloat16).astype(jnp.float32)
    rest = value - high
    mid = rest.astype(jnp.bfloat16).astype(jnp.float32)
    low = (rest - mid).astype(jnp.bfloat16).astype(jnp.float32)
    return high, mid, low


def tail_rows(count, dual, dual_first):
    row = lax.broadcasted_iota(jnp.int32, (16, count), 0)
    high, mid, low = pieces(dual)
    at = 0 if dual_first else 3
    ones_at = 3 - at
    out = jnp.where((row >= ones_at) & (row < ones_at + 3), 1.0, 0.0)
    out = jnp.where(row == at, high, out)
    out = jnp.where(row == at + 1, mid, out)
    return jnp.where(row == at + 2, low, out)


def fill_operands(a_points, a_dual, b_points, b_dual, a_ref, b_ref):
    features = a_points.shape[0]
    a = a_points.astype(jnp.float32)
    cross = 2.0 * KAPPA / features
    rows = jnp.concatenate([a, a, a, tail_rows(a.shape[1], a_dual, False)], axis=0)
    a_ref[...] = rows.T.astype(jnp.bfloat16)
    high, mid, low = pieces(b_points.astype(jnp.float32) * cross)
    b_ref[...] = jnp.concatenate(
        [high, mid, low, tail_rows(high.shape[1], b_dual, True)], axis=0
    ).astype(jnp.bfloat16)


def score_chunk(a_ref, b_ref, at, group):
    return jnp.dot(
        a_ref[at : at + CHUNK, :], b_ref[:, group], preferred_element_type=jnp.float32
    )


def lse_groups(a_ref, b_ref, out_ref):
    def one(n, carry):
        group = pl.ds(pl.multiple_of(n * GROUP, GROUP), GROUP)
        peak = None
        for at in range(0, a_ref.shape[0], CHUNK):
            scores = score_chunk(a_ref, b_ref, at, group).reshape(CHUNK // 8, 8, GROUP)
            here = jnp.max(scores, axis=0)
            if peak is None:
                peak = here
                total = jnp.sum(jnp.exp2(scores - peak[None]), axis=0)
            else:
                risen = jnp.maximum(peak, here)
                total = total * jnp.exp2(peak - risen) + jnp.sum(
                    jnp.exp2(scores - risen[None]), axis=0
                )
                peak = risen
        top = jnp.max(peak, axis=0, keepdims=True)
        total = jnp.sum(total * jnp.exp2(peak - top), axis=0, keepdims=True)
        lse = top + jnp.log(total) * LOG2E
        for d in range(out_ref.shape[0]):
            out_ref[d, :, group] = lse
        return carry

    lax.fori_loop(0, b_ref.shape[1] // GROUP, one, 0)


def sum_groups(a_ref, b_ref, out_ref):
    def one(n, carry):
        group = pl.ds(pl.multiple_of(n * GROUP, GROUP), GROUP)
        total = jnp.zeros((8, GROUP), jnp.float32)
        for at in range(0, a_ref.shape[0], CHUNK):
            scores = score_chunk(a_ref, b_ref, at, group).reshape(CHUNK // 8, 8, GROUP)
            total = total + jnp.sum(jnp.exp2(scores), axis=0)
        total = jnp.sum(total, axis=0, keepdims=True)
        for d in range(out_ref.shape[0]):
            out_ref[d, :, group] = total
        return carry

    lax.fori_loop(0, b_ref.shape[1] // GROUP, one, 0)


def weighted_groups(a_ref, b_ref, points_ref, out_ref, split, exact):
    features = points_ref.shape[0]
    share = features // split

    def one(n, carry):
        group = pl.ds(pl.multiple_of(n * GROUP, GROUP), GROUP)
        total = jnp.zeros((8, GROUP), jnp.float32)
        moved = jnp.zeros((features, GROUP), jnp.float32)
        for at in range(0, a_ref.shape[0], CHUNK):
            weight = jnp.exp2(score_chunk(a_ref, b_ref, at, group))
            total = total + jnp.sum(weight.reshape(CHUNK // 8, 8, GROUP), axis=0)
            points = points_ref[:, at : at + CHUNK]
            rounded = weight.astype(jnp.bfloat16)
            moved = moved + jnp.dot(points, rounded, preferred_element_type=jnp.float32)
            if exact:
                rest = (weight - rounded.astype(jnp.float32)).astype(jnp.bfloat16)
                moved = moved + jnp.dot(points, rest, preferred_element_type=jnp.float32)
        total = jnp.sum(total, axis=0, keepdims=True)
        for part in range(GROUP // LANES):
            lanes = slice(part * LANES, (part + 1) * LANES)
            for h in range(split):
                d = (n * (GROUP // LANES) + part) * split + h
                out_ref[d, :, 0:LANES] = total[:, lanes]
                for k in range(share):
                    out_ref[d, :, (k + 1) * LANES : (k + 2) * LANES] = moved[
                        h * share + k : h * share + k + 1, lanes
                    ]
        return carry

    lax.fori_loop(0, b_ref.shape[1] // GROUP, one, 0)


def norm_of(points_ref):
    points = points_ref[...].astype(jnp.float32)
    return jnp.sum(points * points, axis=0, keepdims=True)


def joined_lse(got_ref):
    parts = [got_ref[d] for d in range(got_ref.shape[0])]
    top = parts[0]
    for part in parts[1:]:
        top = jnp.maximum(top, part)
    total = jnp.exp2(parts[0] - top)
    for part in parts[1:]:
        total = total + jnp.exp2(part - top)
    return top + jnp.log(total) * LOG2E


def joined_sum(got_ref):
    total = got_ref[0]
    for d in range(1, got_ref.shape[0]):
        total = total + got_ref[d]
    return total


def log2_weight(logw_ref, whole):
    return (logw_ref[...] - math.log(whole)) * LOG2E


def first_rows(x_ref, t_ref, out_ref, a_ref, b_ref):
    beta = norm_of(t_ref) * (-KAPPA / t_ref.shape[0])
    zero = jnp.zeros((1, x_ref.shape[1]), jnp.float32)
    fill_operands(t_ref[...], beta, x_ref[...], zero, a_ref, b_ref)
    lse_groups(a_ref, b_ref, out_ref)


def first_cols(whole, x_ref, t_ref, logw_ref, got_ref, alpha_ref, out_ref, a_ref, b_ref):
    alpha = log2_weight(logw_ref, whole) - joined_lse(got_ref)
    alpha_ref[...] = alpha
    zero = jnp.zeros((1, t_ref.shape[1]), jnp.float32)
    fill_operands(x_ref[...], alpha, t_ref[...], zero, a_ref, b_ref)
    lse_groups(a_ref, b_ref, out_ref)


def second_rows(
    whole_s, whole_t, x_ref, t_ref, slogw_ref, tlogw_ref, alpha_ref, got_ref, beta_ref, out_ref, a_ref, b_ref
):
    beta = log2_weight(tlogw_ref, whole_t) - joined_lse(got_ref)
    beta_ref[...] = beta
    over = alpha_ref[...] - log2_weight(slogw_ref, whole_s)
    fill_operands(t_ref[...], beta, x_ref[...], over, a_ref, b_ref)
    sum_groups(a_ref, b_ref, out_ref)


def second_cols(
    whole_t, x_ref, t_ref, tlogw_ref, alpha_ref, beta_ref, got_ref, alpha2_ref, out_ref, a_ref, b_ref
):
    alpha = alpha_ref[...] - jnp.log(joined_sum(got_ref)) * LOG2E
    alpha2_ref[...] = alpha
    over = beta_ref[...] - log2_weight(tlogw_ref, whole_t)
    fill_operands(x_ref[...], alpha, t_ref[...], over, a_ref, b_ref)
    weighted_groups(a_ref, b_ref, x_ref, out_ref, x_ref.shape[0] // HALF, True)


def share_means(got_ref, out_ref):
    total = joined_sum(got_ref)
    mass = total[:, :LANES]
    for d in range(out_ref.shape[0]):
        out_ref[d, :, 0:LANES] = mass
    for at in range(LANES, total.shape[1], LANES):
        mean = total[:, at : at + LANES] / mass
        for d in range(out_ref.shape[0]):
            out_ref[d, :, at : at + LANES] = mean


def unpack_means(got_ref, means_ref, split):
    features = means_ref.shape[0]
    share = features // split
    masses = []
    for d in range(got_ref.shape[0]):
        q, h = divmod(d, split)
        if h == 0:
            masses.append(got_ref[d, :, 0:LANES])
        for k in range(share):
            means_ref[h * share + k : h * share + k + 1, q * LANES : (q + 1) * LANES] = got_ref[
                d, :, (k + 1) * LANES : (k + 2) * LANES
            ]
    return jnp.concatenate(masses, axis=1)


def last_rows(
    x_ref, t_ref, alpha_ref, beta_ref, got_ref, pulled_ref, pot_tgt_ref, out_ref, a_ref, b_ref
):
    mass = unpack_means(got_ref, pulled_ref, x_ref.shape[0] // HALF)
    beta = beta_ref[...] - jnp.log(mass) * LOG2E
    pot_tgt_ref[...] = beta * (1.0 / KAPPA) + norm_of(t_ref) * (1.0 / t_ref.shape[0])
    fill_operands(t_ref[...], beta, x_ref[...], alpha_ref[...], a_ref, b_ref)
    weighted_groups(a_ref, b_ref, t_ref, out_ref, 1, False)


def finish_rows(whole, x_ref, logw_ref, alpha_ref, got_ref, projected_ref, ratio_ref, pot_src_ref):
    mass = unpack_means(got_ref, projected_ref, 1)
    ratio_ref[...] = mass * jnp.exp(math.log(whole) - logw_ref[...]) - 1.0
    pot_src_ref[...] = alpha_ref[...] * (1.0 / KAPPA) + norm_of(x_ref) * (1.0 / x_ref.shape[0])


def call(body, outs, *args, operands=None):
    scratch = []
    if operands is not None:
        scratch = [
            pltpu.VMEM((operands[0], DEPTH), jnp.bfloat16),
            pltpu.VMEM((DEPTH, operands[1]), jnp.bfloat16),
        ]
    return pl.pallas_call(
        body,
        out_shape=[jax.ShapeDtypeStruct(shape, jnp.float32) for shape in outs],
        scratch_shapes=scratch,
        compiler_params=pltpu.CompilerParams(vmem_limit_bytes=32 * 1024 * 1024),
    )(*args)


def spread(parts, axis):
    return lax.all_to_all(parts, axis, 0, 0, tiled=True)


def per_device(x, t, source_logw, target_logw):
    features, rows = x.shape
    cols = t.shape[1]
    n_src, n_tgt = lax.axis_size("src"), lax.axis_size("tgt")
    whole_s, whole_t = rows * n_src, cols * n_tgt
    slogw = source_logw.reshape(1, rows)
    tlogw = target_logw.reshape(1, cols)
    split = features // HALF
    assert n_src * LANES == cols * split and n_tgt * LANES == rows
    col_row = (n_src, 1, (HALF + 1) * LANES)
    row_row = (n_tgt, 1, (features + 1) * LANES)
    by_row, by_col = (cols, rows), (rows, cols)

    (lse,) = call(first_rows, [(n_tgt, 1, rows)], x, t, operands=by_row)
    got = spread(lse, "tgt")

    def body(*refs):
        first_cols(whole_s, *refs)

    alpha, lse = call(body, [(1, rows), (n_src, 1, cols)], x, t, slogw, got, operands=by_col)
    got = spread(lse, "src")

    def body(*refs):
        second_rows(whole_s, whole_t, *refs)

    beta, mass = call(
        body, [(1, cols), (n_tgt, 1, rows)], x, t, slogw, tlogw, alpha, got, operands=by_row
    )
    got = spread(mass, "tgt")

    def body(*refs):
        second_cols(whole_t, *refs)

    alpha, sums = call(
        body, [(1, rows), col_row], x, t, tlogw, alpha, beta, got, operands=by_col
    )
    got = spread(sums, "src")
    (means,) = call(share_means, [col_row], got)
    got = spread(means, "src")
    pulled, pot_tgt, sums = call(
        last_rows, [(features, cols), (1, cols), row_row], x, t, alpha, beta, got, operands=by_row
    )
    got = spread(sums, "tgt")
    (means,) = call(share_means, [row_row], got)
    got = spread(means, "tgt")

    def body(*refs):
        finish_rows(whole_s, *refs)

    projected, ratio, pot_src = call(
        body, [(features, rows), (1, rows), (1, rows)], x, slogw, alpha, got
    )
    return (pot_src.reshape(rows), pot_tgt.reshape(cols), ratio.reshape(rows), projected, pulled)


def solution(mesh):
    in_specs = (P(None, "src"), P(None, "tgt"), P("src"), P("tgt"))
    out_specs = (P("src"), P("tgt"), P("src"), P(None, "src"), P(None, "tgt"))
    return jax.shard_map(
        per_device, mesh=mesh, in_specs=in_specs, out_specs=out_specs, check_vma=False
    )
```

time: 766 us -> 142 us (0.19)
  blocking collectives: 493 us -> 108 us
  waiting for transfers between devices: 159 us -> 0 us
  matrix products: 70.7 us -> 0 us
  Pallas kernels: 0 us -> 30.5 us
  other arithmetic: 17.9 us -> 0 us
  between operations: 14.5 us -> 0.72 us
    psum x6 -> x0, blocking collectives: 286 us -> none  [the longest x2 114 us: col_update(): summed = lax.psum(totals * jnp.exp(peaks - maximum), 'src')]
    pmax x4 -> x0, blocking collectives: 207 us -> none  [the longest x2 125 us: col_update(): maximum = lax.pmax(peaks, 'src')]
    psum x2 -> x0, waiting for transfers between devices: 158 us -> none  [the longest x1 151 us: per_device(): col_total, cmass_total = lax.psum((col_sums, col_mass), 'src')]
    all_to_all x0 -> x7, blocking collectives: none -> 108 us  [spread(): return lax.all_to_all(parts, axis, 0, 0, tiled=True)]
    dot_general x56 -> x0, matrix products: 70.7 us -> none  [the longest x40 65.7 us: cost_block(): lax.dot_general(src_part, target_points, (((0,), (0,)), ((), ())), prefer...]
    pallas_call x0 -> x8, Pallas kernels: none -> 30.5 us  [call(): pl.pallas_call(body, out_shape=[jax.ShapeDtypeStruct(shape, jnp.float32)...]
    reduce_sum x34 -> x0, other arithmetic: 13.7 us -> none  [the longest x16 7.01 us: row_advance(): totals = jnp.sum(jnp.exp(scores - peaks[:, None]), axis=1)]
  transfers between devices with their start and end apart: 2 -> 0, of which waited for: 2 -> 0; matrix products, arithmetic and copies ran while one was open for 0% -> 0% of each run, Pallas kernels for 0% -> 0%
where the time goes in v1:
time: 142 us; the launch traced here: 141 us
  blocking collectives  108 us (76%)
  Pallas kernels  30.5 us (21%)
  local copies, waits for them, and re-layouts  1.7 us (1%)
    all_to_all x7, blocking collectives, spread(): return lax.all_to_all(parts, axis, 0, 0, tiled=True)  108 us
    pallas_call x8, Pallas kernels, call(): pl.pallas_call(body, out_shape=[jax.ShapeDtypeStruct(shape, jnp.float32)...  30.5 us

profile of v1, /device:TPU:1, one launch (start us, length us, event | category | flops | bytes accessed | tf_op | source)
XLA Modules:
  0.0 141.3 jit_solution(4848850485644819337)
XLA Ops:
  0.6 0.0 copy-start
  0.6 0.8 copy-done
  1.5 0.0 copy-start.2
  1.5 0.8 copy-done.2
  2.3 4.9 %shard_map.83 = f32[16,1,2048]{2,1,0:T(1,128)S(1)} custom-call(bf16[16,2048]{1,0:T(8,128)(2,1)S(1)} %copy-done, bf16[16,2048]{1,0:T(8,128)(2,1)S(1)} %copy-done.2), custom_call_target="tpu_custom_call" | custom-call | tf_op jit(solution)/shard_map/pallas_call | solution.py:241
  7.2 0.0 copy-start.4
  7.3 18.5 %all_to_all.35.refs_3_ = f32[16,1,2048]{2,1,0:T(1,128)S(1)} all-to-all(f32[16,1,2048]{2,1,0:T(1,128)S(1)} %shard_map.83), channel_id=1, replica_groups=mesh['src'=32,'tgt'=16] {'tgt'}, dimensions={0} | all-to-all | bytes 262144 | tf_op jit(solution)/shard_map/all_to_all | solution.py:250
  25.8 0.0 copy-done.4
  25.8 5.1 %shard_map.84 = (f32[1,2048]{1,0:T(1,128)S(1)}, f32[32,1,2048]{2,1,0:T(1,128)S(1)}) custom-call(bf16[16,2048]{1,0:T(8,128)(2,1)S(1)} %copy-done, bf16[16,2048]{1,0:T(8,128)(2,1)S(1)} %copy-done.2, f32[1,2048]{1,0:T(1,128)S(1)} %bitcast.5, f32[16,1,2048]{2,1,0:T(1,128)S(1)} %all_to_all.35.refs_3_), custom_call_target="tpu_custom_call" | custom-call | tf_op jit(solution)/shard_map/pallas_call | solution.py:241
  30.8 0.0 copy-start.5
  30.8 22.4 %all_to_all.36.refs_5_ = f32[32,1,2048]{2,1,0:T(1,128)S(1)} all-to-all(f32[32,1,2048]{2,1,0:T(1,128)S(1)} %get-tuple-element.18), channel_id=1, replica_groups=mesh['src'=32,'tgt'=16] {'src'}, dimensions={0} | all-to-all | bytes 524288 | tf_op jit(solution)/shard_map/all_to_all | solution.py:250
  53.3 0.0 copy-done.5
  53.3 3.8 %shard_map.85 = (f32[1,2048]{1,0:T(1,128)S(1)}, f32[16,1,2048]{2,1,0:T(1,128)S(1)}) custom-call(bf16[16,2048]{1,0:T(8,128)(2,1)S(1)} %copy-done, bf16[16,2048]{1,0:T(8,128)(2,1)S(1)} %copy-done.2, f32[1,2048]{1,0:T(1,128)S(1)} %bitcast.6, f32[1,2048]{1,0:T(1,128)S(1)} %bitcast.8, f32[1,2048]{1,0:T(1,128)S(1)} %get-tuple-element.17.refs_4_.refs_3_, ...), custom_call_target="tpu_custom_call" | custom-call | tf_op jit(solution)/shard_map/pallas_call | solution.py:241
  57.1 13.9 %all_to_all.37.refs_5_ = f32[16,1,2048]{2,1,0:T(1,128)S(1)} all-to-all(f32[16,1,2048]{2,1,0:T(1,128)S(1)} %get-tuple-element.20), channel_id=1, replica_groups=mesh['src'=32,'tgt'=16] {'tgt'}, dimensions={0} | all-to-all | bytes 262144 | tf_op jit(solution)/shard_map/all_to_all | solution.py:250
  71.0 7.0 %shard_map.86 = (f32[1,2048]{1,0:T(1,128)S(1)}, f32[32,1,1152]{2,1,0:T(1,128)S(1)}) custom-call(bf16[16,2048]{1,0:T(8,128)(2,1)S(1)} %copy-done, bf16[16,2048]{1,0:T(8,128)(2,1)S(1)} %copy-done.2, f32[1,2048]{1,0:T(1,128)S(1)} %bitcast.9, f32[1,2048]{1,0:T(1,128)S(1)} %get-tuple-element.17.refs_4_.refs_3_, f32[1,2048]{1,0:T(1,128)S(1)} %get-tuple-element.19.refs_4_.beta_ref, ...), custom_call_target="tpu_custom_call" | custom-call | tf_op jit(solution)/shard_map/pallas_call | solution.py:241
  78.0 13.9 %all_to_all.38.got_ref = f32[32,1,1152]{2,1,0:T(1,128)S(1)} all-to-all(f32[32,1,1152]{2,1,0:T(1,128)S(1)} %get-tuple-element.22), channel_id=1, replica_groups=mesh['src'=32,'tgt'=16] {'src'}, dimensions={0} | all-to-all | bytes 294912 | tf_op jit(solution)/shard_map/all_to_all | solution.py:250
  91.9 0.1 shard_map.87
  92.0 0.0 copy-start.1
  92.0 0.0 copy-start.3
  92.0 13.9 %all_to_all.39.got_ref = f32[32,1,1152]{2,1,0:T(1,128)S(1)} all-to-all(f32[32,1,1152]{2,1,0:T(1,128)S(1)} %shard_map.87), channel_id=1, replica_groups=mesh['src'=32,'tgt'=16] {'src'}, dimensions={0} | all-to-all | bytes 294912 | tf_op jit(solution)/shard_map/all_to_all | solution.py:250
  105.9 0.0 copy-done.1
  105.9 0.0 copy-done.3
  105.9 8.8 %shard_map.88 = (f32[16,2048]{1,0:T(8,128)}, f32[1,2048]{1,0:T(1,128)}, f32[16,1,2176]{2,1,0:T(1,128)S(1)}) custom-call(bf16[16,2048]{1,0:T(8,128)(2,1)S(1)} %copy-done.1, bf16[16,2048]{1,0:T(8,128)(2,1)S(1)} %copy-done.3, f32[1,2048]{1,0:T(1,128)S(1)} %get-tuple-element.21.alpha_ref.refs_2_, f32[1,2048]{1,0:T(1,128)S(1)} %get-tuple-element.19.refs_4_.beta_ref, ...), custom_call_target="tpu_custom_call" | custom-call | tf_op jit(solution)/shard_map/pallas_call | solution.py:241
  114.7 14.0 %all_to_all.40.got_ref = f32[16,1,2176]{2,1,0:T(1,128)S(1)} all-to-all(f32[16,1,2176]{2,1,0:T(1,128)S(1)} %get-tuple-element.23), channel_id=1, replica_groups=mesh['src'=32,'tgt'=16] {'tgt'}, dimensions={0} | all-to-all | bytes 278528 | tf_op jit(solution)/shard_map/all_to_all | solution.py:250
  128.7 0.1 shard_map.89
  128.8 11.8 %all_to_all.41.refs_3_ = f32[16,1,2176]{2,1,0:T(1,128)S(1)} all-to-all(f32[16,1,2176]{2,1,0:T(1,128)S(1)} %shard_map.89), channel_id=1, replica_groups=mesh['src'=32,'tgt'=16] {'tgt'}, dimensions={0} | all-to-all | bytes 278528 | tf_op jit(solution)/shard_map/all_to_all | solution.py:250
  140.6 0.7 shard_map.90
Async XLA Ops:
  0.6 0.8 copy-start
  1.5 0.8 copy-start.2
  7.2 18.5 %copy-start.4 = (f32[2048]{0:T(1024)S(1)}, f32[2048]{0:T(1024)}, u32[]{:S(2)}) copy-start(f32[2048]{0:T(1024)} %param.6) | copy-start | bytes 24580
  30.8 22.5 %copy-start.5 = (f32[2048]{0:T(1024)S(1)}, f32[2048]{0:T(1024)}, u32[]{:S(2)}) copy-start(f32[2048]{0:T(1024)} %param.7) | copy-start | bytes 24580
  92.0 13.9 %copy-start.1 = (bf16[16,2048]{1,0:T(8,128)(2,1)S(1)}, bf16[16,2048]{1,0:T(8,128)(2,1)}, u32[]{:S(2)}) copy-start(bf16[16,2048]{1,0:T(8,128)(2,1)} %refs_0_.7) | copy-start | bytes 196612
  92.0 13.9 %copy-start.3 = (bf16[16,2048]{1,0:T(8,128)(2,1)S(1)}, bf16[16,2048]{1,0:T(8,128)(2,1)}, u32[]{:S(2)}) copy-start(bf16[16,2048]{1,0:T(8,128)(2,1)} %t_ref.3) | copy-start | bytes 196612

commit v2 on v1

--- a/solution.py
+++ b/solution.py
@@ -11,8 +11,8 @@
 LOG2E = math.log2(math.e)
 KAPPA = LOG2E / EPSILON
 LANES = 128
-GROUP = 256
 CHUNK = 256
+LSE_CHUNK = 64
 DEPTH = 64
 HALF = 8
 
@@ -48,83 +48,69 @@
     ).astype(jnp.bfloat16)
 
 
-def score_chunk(a_ref, b_ref, at, group):
-    return jnp.dot(
-        a_ref[at : at + CHUNK, :], b_ref[:, group], preferred_element_type=jnp.float32
-    )
-
-
-def lse_groups(a_ref, b_ref, out_ref):
-    def one(n, carry):
-        group = pl.ds(pl.multiple_of(n * GROUP, GROUP), GROUP)
-        peak = None
-        for at in range(0, a_ref.shape[0], CHUNK):
-            scores = score_chunk(a_ref, b_ref, at, group).reshape(CHUNK // 8, 8, GROUP)
-            here = jnp.max(scores, axis=0)
-            if peak is None:
-                peak = here
-                total = jnp.sum(jnp.exp2(scores - peak[None]), axis=0)
-            else:
-                risen = jnp.maximum(peak, here)
-                total = total * jnp.exp2(peak - risen) + jnp.sum(
-                    jnp.exp2(scores - risen[None]), axis=0
-                )
-                peak = risen
-        top = jnp.max(peak, axis=0, keepdims=True)
-        total = jnp.sum(total * jnp.exp2(peak - top), axis=0, keepdims=True)
-        lse = top + jnp.log(total) * LOG2E
-        for d in range(out_ref.shape[0]):
-            out_ref[d, :, group] = lse
-        return carry
-
-    lax.fori_loop(0, b_ref.shape[1] // GROUP, one, 0)
-
-
-def sum_groups(a_ref, b_ref, out_ref):
-    def one(n, carry):
-        group = pl.ds(pl.multiple_of(n * GROUP, GROUP), GROUP)
-        total = jnp.zeros((8, GROUP), jnp.float32)
-        for at in range(0, a_ref.shape[0], CHUNK):
-            scores = score_chunk(a_ref, b_ref, at, group).reshape(CHUNK // 8, 8, GROUP)
-            total = total + jnp.sum(jnp.exp2(scores), axis=0)
-        total = jnp.sum(total, axis=0, keepdims=True)
-        for d in range(out_ref.shape[0]):
-            out_ref[d, :, group] = total
-        return carry
-
-    lax.fori_loop(0, b_ref.shape[1] // GROUP, one, 0)
-
-
-def weighted_groups(a_ref, b_ref, points_ref, out_ref, split, exact):
+def score_chunk(a_ref, b_ref, at, count):
+    return jnp.dot(a_ref[at : at + count, :], b_ref[...], preferred_element_type=jnp.float32)
+
+
+def by_sublane(array):
+    return array.reshape(array.shape[0] // 8, 8, array.shape[1])
+
+
+def lse_columns(a_ref, b_ref, out_ref):
+    peak = None
+    for at in range(0, a_ref.shape[0], LSE_CHUNK):
+        scores = by_sublane(score_chunk(a_ref, b_ref, at, LSE_CHUNK))
+        here = jnp.max(scores, axis=0)
+        if peak is None:
+            peak = here
+            total = jnp.sum(jnp.exp2(scores - peak[None]), axis=0)
+        else:
+            risen = jnp.maximum(peak, here)
+            total = total * jnp.exp2(peak - risen) + jnp.sum(
+                jnp.exp2(scores - risen[None]), axis=0
+            )
+            peak = risen
+    top = jnp.max(peak, axis=0, keepdims=True)
+    total = jnp.sum(total * jnp.exp2(peak - top), axis=0, keepdims=True)
+    lse = top + jnp.log(total) * LOG2E
+    for d in range(out_ref.shape[0]):
+        out_ref[d] = lse
+
+
+def sum_columns(a_ref, b_ref, out_ref):
+    total = jnp.zeros((8, b_ref.shape[1]), jnp.float32)
+    for at in range(0, a_ref.shape[0], CHUNK):
+        total = total + jnp.sum(by_sublane(jnp.exp2(score_chunk(a_ref, b_ref, at, CHUNK))), axis=0)
+    total = jnp.sum(total, axis=0, keepdims=True)
+    for d in range(out_ref.shape[0]):
+        out_ref[d] = total
+
+
+def weighted_columns(a_ref, b_ref, points_ref, out_ref, split, exact):
     features = points_ref.shape[0]
     share = features // split
-
-    def one(n, carry):
-        group = pl.ds(pl.multiple_of(n * GROUP, GROUP), GROUP)
-        total = jnp.zeros((8, GROUP), jnp.float32)
-        moved = jnp.zeros((features, GROUP), jnp.float32)
-        for at in range(0, a_ref.shape[0], CHUNK):
-            weight = jnp.exp2(score_chunk(a_ref, b_ref, at, group))
-            total = total + jnp.sum(weight.reshape(CHUNK // 8, 8, GROUP), axis=0)
-            points = points_ref[:, at : at + CHUNK]
-            rounded = weight.astype(jnp.bfloat16)
-            moved = moved + jnp.dot(points, rounded, preferred_element_type=jnp.float32)
-            if exact:
-                rest = (weight - rounded.astype(jnp.float32)).astype(jnp.bfloat16)
-                moved = moved + jnp.dot(points, rest, preferred_element_type=jnp.float32)
-        total = jnp.sum(total, axis=0, keepdims=True)
-        for part in range(GROUP // LANES):
-            lanes = slice(part * LANES, (part + 1) * LANES)
-            for h in range(split):
-                d = (n * (GROUP // LANES) + part) * split + h
-                out_ref[d, :, 0:LANES] = total[:, lanes]
-                for k in range(share):
-                    out_ref[d, :, (k + 1) * LANES : (k + 2) * LANES] = moved[
-                        h * share + k : h * share + k + 1, lanes
-                    ]
-        return carry
-
-    lax.fori_loop(0, b_ref.shape[1] // GROUP, one, 0)
+    cols = b_ref.shape[1]
+    total = jnp.zeros((8, cols), jnp.float32)
+    moved = jnp.zeros((features, cols), jnp.float32)
+    for at in range(0, a_ref.shape[0], CHUNK):
+        weight = jnp.exp2(score_chunk(a_ref, b_ref, at, CHUNK))
+        total = total + jnp.sum(by_sublane(weight), axis=0)
+        points = points_ref[:, at : at + CHUNK]
+        rounded = weight.astype(jnp.bfloat16)
+        moved = moved + jnp.dot(points, rounded, preferred_element_type=jnp.float32)
+        if exact:
+            rest = (weight - rounded.astype(jnp.float32)).astype(jnp.bfloat16)
+            moved = moved + jnp.dot(points, rest, preferred_element_type=jnp.float32)
+    total = jnp.sum(total, axis=0, keepdims=True)
+    for q in range(cols // LANES):
+        lanes = slice(q * LANES, (q + 1) * LANES)
+        for h in range(split):
+            d = q * split + h
+            out_ref[d, :, 0:LANES] = total[:, lanes]
+            for k in range(share):
+                out_ref[d, :, (k + 1) * LANES : (k + 2) * LANES] = moved[
+                    h * share + k : h * share + k + 1, lanes
+                ]
 
 
 def norm_of(points_ref):
@@ -158,7 +144,7 @@
     beta = norm_of(t_ref) * (-KAPPA / t_ref.shape[0])
     zero = jnp.zeros((1, x_ref.shape[1]), jnp.float32)
     fill_operands(t_ref[...], beta, x_ref[...], zero, a_ref, b_ref)
-    lse_groups(a_ref, b_ref, out_ref)
+    lse_columns(a_ref, b_ref, out_ref)
 
 
 def first_cols(whole, x_ref, t_ref, logw_ref, got_ref, alpha_ref, out_ref, a_ref, b_ref):
@@ -166,7 +152,7 @@
     alpha_ref[...] = alpha
     zero = jnp.zeros((1, t_ref.shape[1]), jnp.float32)
     fill_operands(x_ref[...], alpha, t_ref[...], zero, a_ref, b_ref)
-    lse_groups(a_ref, b_ref, out_ref)
+    lse_columns(a_ref, b_ref, out_ref)
 
 
 def second_rows(
@@ -176,7 +162,7 @@
     beta_ref[...] = beta
     over = alpha_ref[...] - log2_weight(slogw_ref, whole_s)
     fill_operands(t_ref[...], beta, x_ref[...], over, a_ref, b_ref)
-    sum_groups(a_ref, b_ref, out_ref)
+    sum_columns(a_ref, b_ref, out_ref)
 
 
 def second_cols(
@@ -186,7 +172,7 @@
     alpha2_ref[...] = alpha
     over = beta_ref[...] - log2_weight(tlogw_ref, whole_t)
     fill_operands(x_ref[...], alpha, t_ref[...], over, a_ref, b_ref)
-    weighted_groups(a_ref, b_ref, x_ref, out_ref, x_ref.shape[0] // HALF, True)
+    weighted_columns(a_ref, b_ref, x_ref, out_ref, x_ref.shape[0] // HALF, True)
 
 
 def share_means(got_ref, out_ref):
@@ -222,7 +208,7 @@
     beta = beta_ref[...] - jnp.log(mass) * LOG2E
     pot_tgt_ref[...] = beta * (1.0 / KAPPA) + norm_of(t_ref) * (1.0 / t_ref.shape[0])
     fill_operands(t_ref[...], beta, x_ref[...], alpha_ref[...], a_ref, b_ref)
-    weighted_groups(a_ref, b_ref, t_ref, out_ref, 1, False)
+    weighted_columns(a_ref, b_ref, t_ref, out_ref, 1, False)
 
 
 def finish_rows(whole, x_ref, logw_ref, alpha_ref, got_ref, projected_ref, ratio_ref, pot_src_ref):
@@ -242,7 +228,7 @@
         body,
         out_shape=[jax.ShapeDtypeStruct(shape, jnp.float32) for shape in outs],
         scratch_shapes=scratch,
-        compiler_params=pltpu.CompilerParams(vmem_limit_bytes=32 * 1024 * 1024),
+        compiler_params=pltpu.CompilerParams(vmem_limit_bytes=48 * 1024 * 1024),
     )(*args)
 
 

time: 142 us -> 132 us (0.930)
  Pallas kernels: 30.5 us -> 20.4 us
    pallas_call x8, Pallas kernels: 30.5 us -> 20.4 us  [call(): pl.pallas_call(body, out_shape=[jax.ShapeDtypeStruct(shape, jnp.float32)...]
where the time goes in v2:
time: 132 us; the launch traced here: 131 us
  blocking collectives  108 us (82%)
  Pallas kernels  20.4 us (15%)
  local copies, waits for them, and re-layouts  1.7 us (1%)
    all_to_all x7, blocking collectives, spread(): return lax.all_to_all(parts, axis, 0, 0, tiled=True)  108 us
    pallas_call x8, Pallas kernels, call(): pl.pallas_call(body, out_shape=[jax.ShapeDtypeStruct(shape, jnp.float32)...  20.4 us

profile of v2, /device:TPU:1, one launch (start us, length us, event | category | flops | bytes accessed | tf_op | source)
XLA Modules:
  0.0 131.2 jit_solution(10178077712835071235)
XLA Ops:
  0.6 0.0 copy-start
  0.6 0.8 copy-done
  1.5 0.0 copy-start.2
  1.5 0.8 copy-done.2
  2.3 3.6 %shard_map.83 = f32[16,1,2048]{2,1,0:T(1,128)S(1)} custom-call(bf16[16,2048]{1,0:T(8,128)(2,1)S(1)} %copy-done, bf16[16,2048]{1,0:T(8,128)(2,1)S(1)} %copy-done.2), custom_call_target="tpu_custom_call" | custom-call | tf_op jit(solution)/shard_map/pallas_call | solution.py:227
  6.0 0.0 copy-start.4
  6.0 18.5 %all_to_all.35.refs_3_ = f32[16,1,2048]{2,1,0:T(1,128)S(1)} all-to-all(f32[16,1,2048]{2,1,0:T(1,128)S(1)} %shard_map.83), channel_id=1, replica_groups=mesh['src'=32,'tgt'=16] {'tgt'}, dimensions={0} | all-to-all | bytes 262144 | tf_op jit(solution)/shard_map/all_to_all | solution.py:236
  24.5 0.0 copy-done.4
  24.5 3.7 %shard_map.84 = (f32[1,2048]{1,0:T(1,128)S(1)}, f32[32,1,2048]{2,1,0:T(1,128)S(1)}) custom-call(bf16[16,2048]{1,0:T(8,128)(2,1)S(1)} %copy-done, bf16[16,2048]{1,0:T(8,128)(2,1)S(1)} %copy-done.2, f32[1,2048]{1,0:T(1,128)S(1)} %bitcast.5, f32[16,1,2048]{2,1,0:T(1,128)S(1)} %all_to_all.35.refs_3_), custom_call_target="tpu_custom_call" | custom-call | tf_op jit(solution)/shard_map/pallas_call | solution.py:227
  28.2 0.0 copy-start.5
  28.2 22.5 %all_to_all.36.refs_5_ = f32[32,1,2048]{2,1,0:T(1,128)S(1)} all-to-all(f32[32,1,2048]{2,1,0:T(1,128)S(1)} %get-tuple-element.18), channel_id=1, replica_groups=mesh['src'=32,'tgt'=16] {'src'}, dimensions={0} | all-to-all | bytes 524288 | tf_op jit(solution)/shard_map/all_to_all | solution.py:236
  50.7 0.0 copy-done.5
  50.7 2.7 %shard_map.85 = (f32[1,2048]{1,0:T(1,128)S(1)}, f32[16,1,2048]{2,1,0:T(1,128)S(1)}) custom-call(bf16[16,2048]{1,0:T(8,128)(2,1)S(1)} %copy-done, bf16[16,2048]{1,0:T(8,128)(2,1)S(1)} %copy-done.2, f32[1,2048]{1,0:T(1,128)S(1)} %bitcast.6, f32[1,2048]{1,0:T(1,128)S(1)} %bitcast.8, f32[1,2048]{1,0:T(1,128)S(1)} %get-tuple-element.17.refs_4_.refs_3_, ...), custom_call_target="tpu_custom_call" | custom-call | tf_op jit(solution)/shard_map/pallas_call | solution.py:227
  53.4 13.9 %all_to_all.37.refs_5_ = f32[16,1,2048]{2,1,0:T(1,128)S(1)} all-to-all(f32[16,1,2048]{2,1,0:T(1,128)S(1)} %get-tuple-element.20), channel_id=1, replica_groups=mesh['src'=32,'tgt'=16] {'tgt'}, dimensions={0} | all-to-all | bytes 262144 | tf_op jit(solution)/shard_map/all_to_all | solution.py:236
  67.3 5.2 %shard_map.86 = (f32[1,2048]{1,0:T(1,128)S(1)}, f32[32,1,1152]{2,1,0:T(1,128)S(1)}) custom-call(bf16[16,2048]{1,0:T(8,128)(2,1)S(1)} %copy-done, bf16[16,2048]{1,0:T(8,128)(2,1)S(1)} %copy-done.2, f32[1,2048]{1,0:T(1,128)S(1)} %bitcast.9, f32[1,2048]{1,0:T(1,128)S(1)} %get-tuple-element.17.refs_4_.refs_3_, f32[1,2048]{1,0:T(1,128)S(1)} %get-tuple-element.19.refs_4_.beta_ref, ...), custom_call_target="tpu_custom_call" | custom-call | tf_op jit(solution)/shard_map/pallas_call | solution.py:227
  72.5 13.9 %all_to_all.38.got_ref = f32[32,1,1152]{2,1,0:T(1,128)S(1)} all-to-all(f32[32,1,1152]{2,1,0:T(1,128)S(1)} %get-tuple-element.22), channel_id=1, replica_groups=mesh['src'=32,'tgt'=16] {'src'}, dimensions={0} | all-to-all | bytes 294912 | tf_op jit(solution)/shard_map/all_to_all | solution.py:236
  86.4 0.1 shard_map.87
  86.5 0.0 copy-start.1
  86.5 0.0 copy-start.3
  86.5 13.9 %all_to_all.39.got_ref = f32[32,1,1152]{2,1,0:T(1,128)S(1)} all-to-all(f32[32,1,1152]{2,1,0:T(1,128)S(1)} %shard_map.87), channel_id=1, replica_groups=mesh['src'=32,'tgt'=16] {'src'}, dimensions={0} | all-to-all | bytes 294912 | tf_op jit(solution)/shard_map/all_to_all | solution.py:236
  100.4 0.0 copy-done.1
  100.4 0.0 copy-done.3
  100.4 4.3 %shard_map.88 = (f32[16,2048]{1,0:T(8,128)}, f32[1,2048]{1,0:T(1,128)}, f32[16,1,2176]{2,1,0:T(1,128)S(1)}) custom-call(bf16[16,2048]{1,0:T(8,128)(2,1)S(1)} %copy-done.1, bf16[16,2048]{1,0:T(8,128)(2,1)S(1)} %copy-done.3, f32[1,2048]{1,0:T(1,128)S(1)} %get-tuple-element.21.alpha_ref.refs_2_, f32[1,2048]{1,0:T(1,128)S(1)} %get-tuple-element.19.refs_4_.beta_ref, ...), custom_call_target="tpu_custom_call" | custom-call | tf_op jit(solution)/shard_map/pallas_call | solution.py:227
  104.7 14.0 %all_to_all.40.got_ref = f32[16,1,2176]{2,1,0:T(1,128)S(1)} all-to-all(f32[16,1,2176]{2,1,0:T(1,128)S(1)} %get-tuple-element.23), channel_id=1, replica_groups=mesh['src'=32,'tgt'=16] {'tgt'}, dimensions={0} | all-to-all | bytes 278528 | tf_op jit(solution)/shard_map/all_to_all | solution.py:236
  118.7 0.1 shard_map.89
  118.8 11.8 %all_to_all.41.refs_3_ = f32[16,1,2176]{2,1,0:T(1,128)S(1)} all-to-all(f32[16,1,2176]{2,1,0:T(1,128)S(1)} %shard_map.89), channel_id=1, replica_groups=mesh['src'=32,'tgt'=16] {'tgt'}, dimensions={0} | all-to-all | bytes 278528 | tf_op jit(solution)/shard_map/all_to_all | solution.py:236
  130.5 0.7 shard_map.90
Async XLA Ops:
  0.6 0.8 copy-start
  1.5 0.8 copy-start.2
  6.0 18.5 %copy-start.4 = (f32[2048]{0:T(1024)S(1)}, f32[2048]{0:T(1024)}, u32[]{:S(2)}) copy-start(f32[2048]{0:T(1024)} %param.6) | copy-start | bytes 24580
  28.2 22.5 %copy-start.5 = (f32[2048]{0:T(1024)S(1)}, f32[2048]{0:T(1024)}, u32[]{:S(2)}) copy-start(f32[2048]{0:T(1024)} %param.7) | copy-start | bytes 24580
  86.5 13.9 %copy-start.1 = (bf16[16,2048]{1,0:T(8,128)(2,1)S(1)}, bf16[16,2048]{1,0:T(8,128)(2,1)}, u32[]{:S(2)}) copy-start(bf16[16,2048]{1,0:T(8,128)(2,1)} %refs_0_.7) | copy-start | bytes 196612
  86.5 13.9 %copy-start.3 = (bf16[16,2048]{1,0:T(8,128)(2,1)S(1)}, bf16[16,2048]{1,0:T(8,128)(2,1)}, u32[]{:S(2)}) copy-start(bf16[16,2048]{1,0:T(8,128)(2,1)} %t_ref.3) | copy-start | bytes 196612

commit v3 on v2

--- a/solution.py
+++ b/solution.py
@@ -15,6 +15,8 @@
 LSE_CHUNK = 64
 DEPTH = 64
 HALF = 8
+INNER = 8
+SAFE = 2.0**-80
 
 
 def pieces(value):
@@ -56,7 +58,20 @@
     return array.reshape(array.shape[0] // 8, 8, array.shape[1])
 
 
-def lse_columns(a_ref, b_ref, out_ref):
+def lse_columns(a_ref, b_ref, b_dual, out_ref):
+    def store(lse):
+        for d in range(out_ref.shape[0]):
+            out_ref[d] = lse - b_dual
+
+    total = total_of(a_ref, b_ref)
+    store(jnp.log(total) * LOG2E)
+
+    @pl.when(jnp.min(total) < SAFE)
+    def with_peaks():
+        store(lse_of(a_ref, b_ref))
+
+
+def lse_of(a_ref, b_ref):
     peak = None
     for at in range(0, a_ref.shape[0], LSE_CHUNK):
         scores = by_sublane(score_chunk(a_ref, b_ref, at, LSE_CHUNK))
@@ -72,16 +87,18 @@
             peak = risen
     top = jnp.max(peak, axis=0, keepdims=True)
     total = jnp.sum(total * jnp.exp2(peak - top), axis=0, keepdims=True)
-    lse = top + jnp.log(total) * LOG2E
-    for d in range(out_ref.shape[0]):
-        out_ref[d] = lse
-
-
-def sum_columns(a_ref, b_ref, out_ref):
+    return top + jnp.log(total) * LOG2E
+
+
+def total_of(a_ref, b_ref):
     total = jnp.zeros((8, b_ref.shape[1]), jnp.float32)
     for at in range(0, a_ref.shape[0], CHUNK):
         total = total + jnp.sum(by_sublane(jnp.exp2(score_chunk(a_ref, b_ref, at, CHUNK))), axis=0)
-    total = jnp.sum(total, axis=0, keepdims=True)
+    return jnp.sum(total, axis=0, keepdims=True)
+
+
+def sum_columns(a_ref, b_ref, out_ref):
+    total = total_of(a_ref, b_ref)
     for d in range(out_ref.shape[0]):
         out_ref[d] = total
 
@@ -140,19 +157,22 @@
     return (logw_ref[...] - math.log(whole)) * LOG2E
 
 
+def norm_dual(points_ref):
+    return norm_of(points_ref) * (-KAPPA / points_ref.shape[0])
+
+
 def first_rows(x_ref, t_ref, out_ref, a_ref, b_ref):
-    beta = norm_of(t_ref) * (-KAPPA / t_ref.shape[0])
-    zero = jnp.zeros((1, x_ref.shape[1]), jnp.float32)
-    fill_operands(t_ref[...], beta, x_ref[...], zero, a_ref, b_ref)
-    lse_columns(a_ref, b_ref, out_ref)
+    over = norm_dual(x_ref)
+    fill_operands(t_ref[...], norm_dual(t_ref), x_ref[...], over, a_ref, b_ref)
+    lse_columns(a_ref, b_ref, over, out_ref)
 
 
 def first_cols(whole, x_ref, t_ref, logw_ref, got_ref, alpha_ref, out_ref, a_ref, b_ref):
     alpha = log2_weight(logw_ref, whole) - joined_lse(got_ref)
     alpha_ref[...] = alpha
-    zero = jnp.zeros((1, t_ref.shape[1]), jnp.float32)
-    fill_operands(x_ref[...], alpha, t_ref[...], zero, a_ref, b_ref)
-    lse_columns(a_ref, b_ref, out_ref)
+    over = norm_dual(t_ref)
+    fill_operands(x_ref[...], alpha, t_ref[...], over, a_ref, b_ref)
+    lse_columns(a_ref, b_ref, over, out_ref)
 
 
 def second_rows(
@@ -232,8 +252,9 @@
     )(*args)
 
 
-def spread(parts, axis):
-    return lax.all_to_all(parts, axis, 0, 0, tiled=True)
+def spread(parts, axis, order=None):
+    groups = None if order is None else [order]
+    return lax.all_to_all(parts, axis, 0, 0, axis_index_groups=groups, tiled=True)
 
 
 def per_device(x, t, source_logw, target_logw):
@@ -244,6 +265,7 @@
     slogw = source_logw.reshape(1, rows)
     tlogw = target_logw.reshape(1, cols)
     split = features // HALF
+    order = [(r % (n_src // INNER)) * INNER + r // (n_src // INNER) for r in range(n_src)]
     assert n_src * LANES == cols * split and n_tgt * LANES == rows
     col_row = (n_src, 1, (HALF + 1) * LANES)
     row_row = (n_tgt, 1, (features + 1) * LANES)
@@ -256,7 +278,7 @@
         first_cols(whole_s, *refs)
 
     alpha, lse = call(body, [(1, rows), (n_src, 1, cols)], x, t, slogw, got, operands=by_col)
-    got = spread(lse, "src")
+    got = spread(lse, "src", order)
 
     def body(*refs):
         second_rows(whole_s, whole_t, *refs)
@@ -272,9 +294,9 @@
     alpha, sums = call(
         body, [(1, rows), col_row], x, t, tlogw, alpha, beta, got, operands=by_col
     )
-    got = spread(sums, "src")
+    got = spread(sums, "src", order)
     (means,) = call(share_means, [col_row], got)
-    got = spread(means, "src")
+    got = spread(means, "src", order)
     pulled, pot_tgt, sums = call(
         last_rows, [(features, cols), (1, cols), row_row], x, t, alpha, beta, got, operands=by_row
     )

time: 132 us -> 136 us (1.030)
  Pallas kernels: 20.4 us -> 25 us
    pallas_call x8, Pallas kernels: 20.4 us -> 25 us  [call(): pl.pallas_call(body, out_shape=[jax.ShapeDtypeStruct(shape, jnp.float32)...]
where the time goes in v3:
time: 136 us
  blocking collectives  109 us (80%)
  Pallas kernels  25 us (18%)
  local copies, waits for them, and re-layouts  1.7 us (1%)
    all_to_all x7, blocking collectives, spread(): lax.all_to_all(parts, axis, 0, 0, axis_index_groups=groups, tiled=True)  109 us
    pallas_call x8, Pallas kernels, call(): pl.pallas_call(body, out_shape=[jax.ShapeDtypeStruct(shape, jnp.float32)...  25 us

profile of v3, /device:TPU:1, one launch (start us, length us, event | category | flops | bytes accessed | tf_op | source)
XLA Modules:
  0.0 136.0 jit_solution(2753689095112641457)
XLA Ops:
  0.6 0.0 copy-start
  0.6 0.8 copy-done
  1.5 0.0 copy-start.2
  1.5 0.8 copy-done.2
  2.3 5.8 %shard_map.83 = f32[16,1,2048]{2,1,0:T(1,128)S(1)} custom-call(bf16[16,2048]{1,0:T(8,128)(2,1)S(1)} %copy-done, bf16[16,2048]{1,0:T(8,128)(2,1)S(1)} %copy-done.2), custom_call_target="tpu_custom_call" | custom-call | tf_op jit(solution)/shard_map/pallas_call | solution.py:247
  8.1 0.0 copy-start.4
  8.1 18.5 %all_to_all.35.refs_3_ = f32[16,1,2048]{2,1,0:T(1,128)S(1)} all-to-all(f32[16,1,2048]{2,1,0:T(1,128)S(1)} %shard_map.83), channel_id=1, replica_groups=mesh['src'=32,'tgt'=16] {'tgt'}, dimensions={0} | all-to-all | bytes 262144 | tf_op jit(solution)/shard_map/all_to_all | solution.py:257
  26.6 0.0 copy-done.4
  26.6 6.1 %shard_map.84 = (f32[1,2048]{1,0:T(1,128)S(1)}, f32[32,1,2048]{2,1,0:T(1,128)S(1)}) custom-call(bf16[16,2048]{1,0:T(8,128)(2,1)S(1)} %copy-done, bf16[16,2048]{1,0:T(8,128)(2,1)S(1)} %copy-done.2, f32[1,2048]{1,0:T(1,128)S(1)} %bitcast.5, f32[16,1,2048]{2,1,0:T(1,128)S(1)} %all_to_all.35.refs_3_), custom_call_target="tpu_custom_call" | custom-call | tf_op jit(solution)/shard_map/pallas_call | solution.py:247
  32.8 0.0 copy-start.5
  32.8 24.0 %all_to_all.36.refs_5_ = f32[32,1,2048]{2,1,0:T(1,128)S(1)} all-to-all(f32[32,1,2048]{2,1,0:T(1,128)S(1)} %get-tuple-element.18), channel_id=1, replica_groups={{0,128,256,384,16,144,272,400,32,160,288,416,48,176,304,432,64,192,320,..., dimensions={0} | all-to-all | bytes 524288 | tf_op jit(solution)/shard_map/all_to_all | solution.py:257
  56.8 0.0 copy-done.5
  56.8 2.7 %shard_map.85 = (f32[1,2048]{1,0:T(1,128)S(1)}, f32[16,1,2048]{2,1,0:T(1,128)S(1)}) custom-call(bf16[16,2048]{1,0:T(8,128)(2,1)S(1)} %copy-done, bf16[16,2048]{1,0:T(8,128)(2,1)S(1)} %copy-done.2, f32[1,2048]{1,0:T(1,128)S(1)} %bitcast.6, f32[1,2048]{1,0:T(1,128)S(1)} %bitcast.8, f32[1,2048]{1,0:T(1,128)S(1)} %get-tuple-element.17.refs_4_.refs_3_, ...), custom_call_target="tpu_custom_call" | custom-call | tf_op jit(solution)/shard_map/pallas_call | solution.py:247
  59.5 13.2 %all_to_all.37.refs_5_ = f32[16,1,2048]{2,1,0:T(1,128)S(1)} all-to-all(f32[16,1,2048]{2,1,0:T(1,128)S(1)} %get-tuple-element.20), channel_id=1, replica_groups=mesh['src'=32,'tgt'=16] {'tgt'}, dimensions={0} | all-to-all | bytes 262144 | tf_op jit(solution)/shard_map/all_to_all | solution.py:257
  72.7 5.2 %shard_map.86 = (f32[1,2048]{1,0:T(1,128)S(1)}, f32[32,1,1152]{2,1,0:T(1,128)S(1)}) custom-call(bf16[16,2048]{1,0:T(8,128)(2,1)S(1)} %copy-done, bf16[16,2048]{1,0:T(8,128)(2,1)S(1)} %copy-done.2, f32[1,2048]{1,0:T(1,128)S(1)} %bitcast.9, f32[1,2048]{1,0:T(1,128)S(1)} %get-tuple-element.17.refs_4_.refs_3_, f32[1,2048]{1,0:T(1,128)S(1)} %get-tuple-element.19.refs_4_.beta_ref, ...), custom_call_target="tpu_custom_call" | custom-call | tf_op jit(solution)/shard_map/pallas_call | solution.py:247
  78.0 13.6 %all_to_all.38.got_ref = f32[32,1,1152]{2,1,0:T(1,128)S(1)} all-to-all(f32[32,1,1152]{2,1,0:T(1,128)S(1)} %get-tuple-element.22), channel_id=1, replica_groups={{0,128,256,384,16,144,272,400,32,160,288,416,48,176,304,432,64,192,320,..., dimensions={0} | all-to-all | bytes 294912 | tf_op jit(solution)/shard_map/all_to_all | solution.py:257
  91.5 0.1 shard_map.87
  91.6 0.0 copy-start.1
  91.6 0.0 copy-start.3
  91.7 13.1 %all_to_all.39.got_ref = f32[32,1,1152]{2,1,0:T(1,128)S(1)} all-to-all(f32[32,1,1152]{2,1,0:T(1,128)S(1)} %shard_map.87), channel_id=1, replica_groups={{0,128,256,384,16,144,272,400,32,160,288,416,48,176,304,432,64,192,320,..., dimensions={0} | all-to-all | bytes 294912 | tf_op jit(solution)/shard_map/all_to_all | solution.py:257
  104.8 0.0 copy-done.1
  104.8 0.0 copy-done.3
  104.8 4.3 %shard_map.88 = (f32[16,2048]{1,0:T(8,128)}, f32[1,2048]{1,0:T(1,128)}, f32[16,1,2176]{2,1,0:T(1,128)S(1)}) custom-call(bf16[16,2048]{1,0:T(8,128)(2,1)S(1)} %copy-done.1, bf16[16,2048]{1,0:T(8,128)(2,1)S(1)} %copy-done.3, f32[1,2048]{1,0:T(1,128)S(1)} %get-tuple-element.21.alpha_ref.refs_2_, f32[1,2048]{1,0:T(1,128)S(1)} %get-tuple-element.19.refs_4_.beta_ref, ...), custom_call_target="tpu_custom_call" | custom-call | tf_op jit(solution)/shard_map/pallas_call | solution.py:247
  109.0 14.4 %all_to_all.40.got_ref = f32[16,1,2176]{2,1,0:T(1,128)S(1)} all-to-all(f32[16,1,2176]{2,1,0:T(1,128)S(1)} %get-tuple-element.23), channel_id=1, replica_groups=mesh['src'=32,'tgt'=16] {'tgt'}, dimensions={0} | all-to-all | bytes 278528 | tf_op jit(solution)/shard_map/all_to_all | solution.py:257
  123.4 0.1 shard_map.89
  123.5 11.8 %all_to_all.41.refs_3_ = f32[16,1,2176]{2,1,0:T(1,128)S(1)} all-to-all(f32[16,1,2176]{2,1,0:T(1,128)S(1)} %shard_map.89), channel_id=1, replica_groups=mesh['src'=32,'tgt'=16] {'tgt'}, dimensions={0} | all-to-all | bytes 278528 | tf_op jit(solution)/shard_map/all_to_all | solution.py:257
  135.3 0.7 shard_map.90
Async XLA Ops:
  0.6 0.8 copy-start
  1.5 0.8 copy-start.2
  8.1 18.5 %copy-start.4 = (f32[2048]{0:T(1024)S(1)}, f32[2048]{0:T(1024)}, u32[]{:S(2)}) copy-start(f32[2048]{0:T(1024)} %param.6) | copy-start | bytes 24580
  32.8 24.0 %copy-start.5 = (f32[2048]{0:T(1024)S(1)}, f32[2048]{0:T(1024)}, u32[]{:S(2)}) copy-start(f32[2048]{0:T(1024)} %param.7) | copy-start | bytes 24580
  91.6 13.1 %copy-start.1 = (bf16[16,2048]{1,0:T(8,128)(2,1)S(1)}, bf16[16,2048]{1,0:T(8,128)(2,1)}, u32[]{:S(2)}) copy-start(bf16[16,2048]{1,0:T(8,128)(2,1)} %refs_0_.7) | copy-start | bytes 196612
  91.6 13.1 %copy-start.3 = (bf16[16,2048]{1,0:T(8,128)(2,1)S(1)}, bf16[16,2048]{1,0:T(8,128)(2,1)}, u32[]{:S(2)}) copy-start(bf16[16,2048]{1,0:T(8,128)(2,1)} %t_ref.3) | copy-start | bytes 196612

commit v4 on v3

--- a/solution.py
+++ b/solution.py
@@ -16,6 +16,7 @@
 DEPTH = 64
 HALF = 8
 INNER = 8
+FIRST = 5
 SAFE = 2.0**-80
 
 
@@ -252,9 +253,8 @@
     )(*args)
 
 
-def spread(parts, axis, order=None):
-    groups = None if order is None else [order]
-    return lax.all_to_all(parts, axis, 0, 0, axis_index_groups=groups, tiled=True)
+def spread(parts, axis, order):
+    return lax.all_to_all(parts, axis, 0, 0, axis_index_groups=[order], tiled=True)
 
 
 def per_device(x, t, source_logw, target_logw):
@@ -265,20 +265,22 @@
     slogw = source_logw.reshape(1, rows)
     tlogw = target_logw.reshape(1, cols)
     split = features // HALF
-    order = [(r % (n_src // INNER)) * INNER + r // (n_src // INNER) for r in range(n_src)]
+    outer = n_src // INNER
+    by_src = [(r + outer // 2) % outer * INNER + (r // outer + FIRST) % INNER for r in range(n_src)]
+    by_tgt = [(r + n_tgt // 2) % n_tgt for r in range(n_tgt)]
     assert n_src * LANES == cols * split and n_tgt * LANES == rows
     col_row = (n_src, 1, (HALF + 1) * LANES)
     row_row = (n_tgt, 1, (features + 1) * LANES)
     by_row, by_col = (cols, rows), (rows, cols)
 
     (lse,) = call(first_rows, [(n_tgt, 1, rows)], x, t, operands=by_row)
-    got = spread(lse, "tgt")
+    got = spread(lse, "tgt", by_tgt)
 
     def body(*refs):
         first_cols(whole_s, *refs)
 
     alpha, lse = call(body, [(1, rows), (n_src, 1, cols)], x, t, slogw, got, operands=by_col)
-    got = spread(lse, "src", order)
+    got = spread(lse, "src", by_src)
 
     def body(*refs):
         second_rows(whole_s, whole_t, *refs)
@@ -286,7 +288,7 @@
     beta, mass = call(
         body, [(1, cols), (n_tgt, 1, rows)], x, t, slogw, tlogw, alpha, got, operands=by_row
     )
-    got = spread(mass, "tgt")
+    got = spread(mass, "tgt", by_tgt)
 
     def body(*refs):
         second_cols(whole_t, *refs)
@@ -294,15 +296,15 @@
     alpha, sums = call(
         body, [(1, rows), col_row], x, t, tlogw, alpha, beta, got, operands=by_col
     )
-    got = spread(sums, "src", order)
+    got = spread(sums, "src", by_src)
     (means,) = call(share_means, [col_row], got)
-    got = spread(means, "src", order)
+    got = spread(means, "src", by_src)
     pulled, pot_tgt, sums = call(
         last_rows, [(features, cols), (1, cols), row_row], x, t, alpha, beta, got, operands=by_row
     )
-    got = spread(sums, "tgt")
+    got = spread(sums, "tgt", by_tgt)
     (means,) = call(share_means, [row_row], got)
-    got = spread(means, "tgt")
+    got = spread(means, "tgt", by_tgt)
 
     def body(*refs):
         finish_rows(whole_s, *refs)

time: 136 us -> 129 us (0.949)
  blocking collectives: 109 us -> 101 us
    all_to_all x7, blocking collectives: 109 us -> 101 us  [spread(): lax.all_to_all(parts, axis, 0, 0, axis_index_groups=[order], tiled=True)]
where the time goes in v4:
time: 129 us
  blocking collectives  101 us (78%)
  Pallas kernels  25 us (19%)
  local copies, waits for them, and re-layouts  1.7 us (1%)
    all_to_all x7, blocking collectives, spread(): lax.all_to_all(parts, axis, 0, 0, axis_index_groups=[order], tiled=True)  101 us
    pallas_call x8, Pallas kernels, call(): pl.pallas_call(body, out_shape=[jax.ShapeDtypeStruct(shape, jnp.float32)...  25 us

profile of v4, /device:TPU:1, one launch (start us, length us, event | category | flops | bytes accessed | tf_op | source)
XLA Modules:
  0.0 128.8 jit_solution(18048058375683613592)
XLA Ops:
  0.6 0.0 copy-start
  0.6 0.8 copy-done
  1.5 0.0 copy-start.2
  1.5 0.8 copy-done.2
  2.3 5.8 %shard_map.83 = f32[16,1,2048]{2,1,0:T(1,128)S(1)} custom-call(bf16[16,2048]{1,0:T(8,128)(2,1)S(1)} %copy-done, bf16[16,2048]{1,0:T(8,128)(2,1)S(1)} %copy-done.2), custom_call_target="tpu_custom_call" | custom-call | tf_op jit(solution)/shard_map/pallas_call | solution.py:248
  8.1 0.0 copy-start.4
  8.1 18.1 %all_to_all.35.refs_3_ = f32[16,1,2048]{2,1,0:T(1,128)S(1)} all-to-all(f32[16,1,2048]{2,1,0:T(1,128)S(1)} %shard_map.83), channel_id=1, replica_groups={{8,9,10,11,12,13,14,15,0,1,2,3,4,5,6,7},{24,25,26,27,28,29,30,31,16,17,..., dimensions={0} | all-to-all | bytes 262144 | tf_op jit(solution)/shard_map/all_to_all | solution.py:257
  26.2 0.0 copy-done.4
  26.2 6.1 %shard_map.84 = (f32[1,2048]{1,0:T(1,128)S(1)}, f32[32,1,2048]{2,1,0:T(1,128)S(1)}) custom-call(bf16[16,2048]{1,0:T(8,128)(2,1)S(1)} %copy-done, bf16[16,2048]{1,0:T(8,128)(2,1)S(1)} %copy-done.2, f32[1,2048]{1,0:T(1,128)S(1)} %bitcast.5, f32[16,1,2048]{2,1,0:T(1,128)S(1)} %all_to_all.35.refs_3_), custom_call_target="tpu_custom_call" | custom-call | tf_op jit(solution)/shard_map/pallas_call | solution.py:248
  32.3 0.0 copy-start.5
  32.4 17.7 %all_to_all.36.refs_5_ = f32[32,1,2048]{2,1,0:T(1,128)S(1)} all-to-all(f32[32,1,2048]{2,1,0:T(1,128)S(1)} %get-tuple-element.18), channel_id=1, replica_groups={{336,464,80,208,352,480,96,224,368,496,112,240,256,384,0,128,272,400,16..., dimensions={0} | all-to-all | bytes 524288 | tf_op jit(solution)/shard_map/all_to_all | solution.py:257
  50.0 0.0 copy-done.5
  50.0 2.7 %shard_map.85 = (f32[1,2048]{1,0:T(1,128)S(1)}, f32[16,1,2048]{2,1,0:T(1,128)S(1)}) custom-call(bf16[16,2048]{1,0:T(8,128)(2,1)S(1)} %copy-done, bf16[16,2048]{1,0:T(8,128)(2,1)S(1)} %copy-done.2, f32[1,2048]{1,0:T(1,128)S(1)} %bitcast.6, f32[1,2048]{1,0:T(1,128)S(1)} %bitcast.8, f32[1,2048]{1,0:T(1,128)S(1)} %get-tuple-element.17.refs_4_.refs_3_, ...), custom_call_target="tpu_custom_call" | custom-call | tf_op jit(solution)/shard_map/pallas_call | solution.py:248
  52.7 13.2 %all_to_all.37.refs_5_ = f32[16,1,2048]{2,1,0:T(1,128)S(1)} all-to-all(f32[16,1,2048]{2,1,0:T(1,128)S(1)} %get-tuple-element.20), channel_id=1, replica_groups={{8,9,10,11,12,13,14,15,0,1,2,3,4,5,6,7},{24,25,26,27,28,29,30,31,16,17,..., dimensions={0} | all-to-all | bytes 262144 | tf_op jit(solution)/shard_map/all_to_all | solution.py:257
  65.9 5.2 %shard_map.86 = (f32[1,2048]{1,0:T(1,128)S(1)}, f32[32,1,1152]{2,1,0:T(1,128)S(1)}) custom-call(bf16[16,2048]{1,0:T(8,128)(2,1)S(1)} %copy-done, bf16[16,2048]{1,0:T(8,128)(2,1)S(1)} %copy-done.2, f32[1,2048]{1,0:T(1,128)S(1)} %bitcast.9, f32[1,2048]{1,0:T(1,128)S(1)} %get-tuple-element.17.refs_4_.refs_3_, f32[1,2048]{1,0:T(1,128)S(1)} %get-tuple-element.19.refs_4_.beta_ref, ...), custom_call_target="tpu_custom_call" | custom-call | tf_op jit(solution)/shard_map/pallas_call | solution.py:248
  71.1 13.4 %all_to_all.38.got_ref = f32[32,1,1152]{2,1,0:T(1,128)S(1)} all-to-all(f32[32,1,1152]{2,1,0:T(1,128)S(1)} %get-tuple-element.22), channel_id=1, replica_groups={{336,464,80,208,352,480,96,224,368,496,112,240,256,384,0,128,272,400,16..., dimensions={0} | all-to-all | bytes 294912 | tf_op jit(solution)/shard_map/all_to_all | solution.py:257
  84.6 0.1 shard_map.87
  84.7 0.0 copy-start.1
  84.7 0.0 copy-start.3
  84.7 12.8 %all_to_all.39.got_ref = f32[32,1,1152]{2,1,0:T(1,128)S(1)} all-to-all(f32[32,1,1152]{2,1,0:T(1,128)S(1)} %shard_map.87), channel_id=1, replica_groups={{336,464,80,208,352,480,96,224,368,496,112,240,256,384,0,128,272,400,16..., dimensions={0} | all-to-all | bytes 294912 | tf_op jit(solution)/shard_map/all_to_all | solution.py:257
  97.5 0.0 copy-done.1
  97.5 0.0 copy-done.3
  97.5 4.3 %shard_map.88 = (f32[16,2048]{1,0:T(8,128)}, f32[1,2048]{1,0:T(1,128)}, f32[16,1,2176]{2,1,0:T(1,128)S(1)}) custom-call(bf16[16,2048]{1,0:T(8,128)(2,1)S(1)} %copy-done.1, bf16[16,2048]{1,0:T(8,128)(2,1)S(1)} %copy-done.3, f32[1,2048]{1,0:T(1,128)S(1)} %get-tuple-element.21.alpha_ref.refs_2_, f32[1,2048]{1,0:T(1,128)S(1)} %get-tuple-element.19.refs_4_.beta_ref, ...), custom_call_target="tpu_custom_call" | custom-call | tf_op jit(solution)/shard_map/pallas_call | solution.py:248
  101.8 14.5 %all_to_all.40.got_ref = f32[16,1,2176]{2,1,0:T(1,128)S(1)} all-to-all(f32[16,1,2176]{2,1,0:T(1,128)S(1)} %get-tuple-element.23), channel_id=1, replica_groups={{8,9,10,11,12,13,14,15,0,1,2,3,4,5,6,7},{24,25,26,27,28,29,30,31,16,17,..., dimensions={0} | all-to-all | bytes 278528 | tf_op jit(solution)/shard_map/all_to_all | solution.py:257
  116.3 0.1 shard_map.89
  116.3 11.8 %all_to_all.41.refs_3_ = f32[16,1,2176]{2,1,0:T(1,128)S(1)} all-to-all(f32[16,1,2176]{2,1,0:T(1,128)S(1)} %shard_map.89), channel_id=1, replica_groups={{8,9,10,11,12,13,14,15,0,1,2,3,4,5,6,7},{24,25,26,27,28,29,30,31,16,17,..., dimensions={0} | all-to-all | bytes 278528 | tf_op jit(solution)/shard_map/all_to_all | solution.py:257
  128.2 0.7 shard_map.90
Async XLA Ops:
  0.6 0.8 copy-start
  1.5 0.8 copy-start.2
  8.1 18.1 %copy-start.4 = (f32[2048]{0:T(1024)S(1)}, f32[2048]{0:T(1024)}, u32[]{:S(2)}) copy-start(f32[2048]{0:T(1024)} %param.6) | copy-start | bytes 24580
  32.3 17.7 %copy-start.5 = (f32[2048]{0:T(1024)S(1)}, f32[2048]{0:T(1024)}, u32[]{:S(2)}) copy-start(f32[2048]{0:T(1024)} %param.7) | copy-start | bytes 24580
  84.7 12.9 %copy-start.1 = (bf16[16,2048]{1,0:T(8,128)(2,1)S(1)}, bf16[16,2048]{1,0:T(8,128)(2,1)}, u32[]{:S(2)}) copy-start(bf16[16,2048]{1,0:T(8,128)(2,1)} %refs_0_.7) | copy-start | bytes 196612
  84.7 12.9 %copy-start.3 = (bf16[16,2048]{1,0:T(8,128)(2,1)S(1)}, bf16[16,2048]{1,0:T(8,128)(2,1)}, u32[]{:S(2)}) copy-start(bf16[16,2048]{1,0:T(8,128)(2,1)} %t_ref.3) | copy-start | bytes 196612

commit v5 on v4

--- a/solution.py
+++ b/solution.py
@@ -158,17 +158,24 @@
     return (logw_ref[...] - math.log(whole)) * LOG2E
 
 
+def clouds(xt_ref):
+    features = xt_ref.shape[0] // 2
+    return xt_ref.at[:features], xt_ref.at[features:]
+
+
 def norm_dual(points_ref):
     return norm_of(points_ref) * (-KAPPA / points_ref.shape[0])
 
 
-def first_rows(x_ref, t_ref, out_ref, a_ref, b_ref):
+def first_rows(xt_ref, out_ref, a_ref, b_ref):
+    x_ref, t_ref = clouds(xt_ref)
     over = norm_dual(x_ref)
     fill_operands(t_ref[...], norm_dual(t_ref), x_ref[...], over, a_ref, b_ref)
     lse_columns(a_ref, b_ref, over, out_ref)
 
 
-def first_cols(whole, x_ref, t_ref, logw_ref, got_ref, alpha_ref, out_ref, a_ref, b_ref):
+def first_cols(whole, xt_ref, logw_ref, got_ref, alpha_ref, out_ref, a_ref, b_ref):
+    x_ref, t_ref = clouds(xt_ref)
     alpha = log2_weight(logw_ref, whole) - joined_lse(got_ref)
     alpha_ref[...] = alpha
     over = norm_dual(t_ref)
@@ -177,8 +184,9 @@
 
 
 def second_rows(
-    whole_s, whole_t, x_ref, t_ref, slogw_ref, tlogw_ref, alpha_ref, got_ref, beta_ref, out_ref, a_ref, b_ref
+    whole_s, whole_t, xt_ref, slogw_ref, tlogw_ref, alpha_ref, got_ref, beta_ref, out_ref, a_ref, b_ref
 ):
+    x_ref, t_ref = clouds(xt_ref)
     beta = log2_weight(tlogw_ref, whole_t) - joined_lse(got_ref)
     beta_ref[...] = beta
     over = alpha_ref[...] - log2_weight(slogw_ref, whole_s)
@@ -187,8 +195,9 @@
 
 
 def second_cols(
-    whole_t, x_ref, t_ref, tlogw_ref, alpha_ref, beta_ref, got_ref, alpha2_ref, out_ref, a_ref, b_ref
+    whole_t, xt_ref, tlogw_ref, alpha_ref, beta_ref, got_ref, alpha2_ref, out_ref, a_ref, b_ref
 ):
+    x_ref, t_ref = clouds(xt_ref)
     alpha = alpha_ref[...] - jnp.log(joined_sum(got_ref)) * LOG2E
     alpha2_ref[...] = alpha
     over = beta_ref[...] - log2_weight(tlogw_ref, whole_t)
@@ -223,8 +232,9 @@
 
 
 def last_rows(
-    x_ref, t_ref, alpha_ref, beta_ref, got_ref, pulled_ref, pot_tgt_ref, out_ref, a_ref, b_ref
+    xt_ref, alpha_ref, beta_ref, got_ref, pulled_ref, pot_tgt_ref, out_ref, a_ref, b_ref
 ):
+    x_ref, t_ref = clouds(xt_ref)
     mass = unpack_means(got_ref, pulled_ref, x_ref.shape[0] // HALF)
     beta = beta_ref[...] - jnp.log(mass) * LOG2E
     pot_tgt_ref[...] = beta * (1.0 / KAPPA) + norm_of(t_ref) * (1.0 / t_ref.shape[0])
@@ -232,7 +242,8 @@
     weighted_columns(a_ref, b_ref, t_ref, out_ref, 1, False)
 
 
-def finish_rows(whole, x_ref, logw_ref, alpha_ref, got_ref, projected_ref, ratio_ref, pot_src_ref):
+def finish_rows(whole, xt_ref, logw_ref, alpha_ref, got_ref, projected_ref, ratio_ref, pot_src_ref):
+    x_ref, _ = clouds(xt_ref)
     mass = unpack_means(got_ref, projected_ref, 1)
     ratio_ref[...] = mass * jnp.exp(math.log(whole) - logw_ref[...]) - 1.0
     pot_src_ref[...] = alpha_ref[...] * (1.0 / KAPPA) + norm_of(x_ref) * (1.0 / x_ref.shape[0])
@@ -265,28 +276,29 @@
     slogw = source_logw.reshape(1, rows)
     tlogw = target_logw.reshape(1, cols)
     split = features // HALF
+    xt = jnp.concatenate([x, t], axis=0)
     outer = n_src // INNER
     by_src = [(r + outer // 2) % outer * INNER + (r // outer + FIRST) % INNER for r in range(n_src)]
     by_tgt = [(r + n_tgt // 2) % n_tgt for r in range(n_tgt)]
-    assert n_src * LANES == cols * split and n_tgt * LANES == rows
+    assert rows == cols and n_src * LANES == cols * split and n_tgt * LANES == rows
     col_row = (n_src, 1, (HALF + 1) * LANES)
     row_row = (n_tgt, 1, (features + 1) * LANES)
     by_row, by_col = (cols, rows), (rows, cols)
 
-    (lse,) = call(first_rows, [(n_tgt, 1, rows)], x, t, operands=by_row)
+    (lse,) = call(first_rows, [(n_tgt, 1, rows)], xt, operands=by_row)
     got = spread(lse, "tgt", by_tgt)
 
     def body(*refs):
         first_cols(whole_s, *refs)
 
-    alpha, lse = call(body, [(1, rows), (n_src, 1, cols)], x, t, slogw, got, operands=by_col)
+    alpha, lse = call(body, [(1, rows), (n_src, 1, cols)], xt, slogw, got, operands=by_col)
     got = spread(lse, "src", by_src)
 
     def body(*refs):
         second_rows(whole_s, whole_t, *refs)
 
     beta, mass = call(
-        body, [(1, cols), (n_tgt, 1, rows)], x, t, slogw, tlogw, alpha, got, operands=by_row
+        body, [(1, cols), (n_tgt, 1, rows)], xt, slogw, tlogw, alpha, got, operands=by_row
     )
     got = spread(mass, "tgt", by_tgt)
 
@@ -294,13 +306,13 @@
         second_cols(whole_t, *refs)
 
     alpha, sums = call(
-        body, [(1, rows), col_row], x, t, tlogw, alpha, beta, got, operands=by_col
+        body, [(1, rows), col_row], xt, tlogw, alpha, beta, got, operands=by_col
     )
     got = spread(sums, "src", by_src)
     (means,) = call(share_means, [col_row], got)
     got = spread(means, "src", by_src)
     pulled, pot_tgt, sums = call(
-        last_rows, [(features, cols), (1, cols), row_row], x, t, alpha, beta, got, operands=by_row
+        last_rows, [(features, cols), (1, cols), row_row], xt, alpha, beta, got, operands=by_row
     )
     got = spread(sums, "tgt", by_tgt)
     (means,) = call(share_means, [row_row], got)
@@ -310,7 +322,7 @@
         finish_rows(whole_s, *refs)
 
     projected, ratio, pot_src = call(
-        body, [(features, rows), (1, rows), (1, rows)], x, slogw, alpha, got
+        body, [(features, rows), (1, rows), (1, rows)], xt, slogw, alpha, got
     )
     return (pot_src.reshape(rows), pot_tgt.reshape(cols), ratio.reshape(rows), projected, pulled)
 

time: 129 us -> 128 us (level)
  no operation moved by 1% of the time
where the time goes in v5:
time: 128 us
  blocking collectives  101 us (79%)
  Pallas kernels  25 us (20%)
    all_to_all x7, blocking collectives, spread(): lax.all_to_all(parts, axis, 0, 0, axis_index_groups=[order], tiled=True)  101 us
    pallas_call x8, Pallas kernels, call(): pl.pallas_call(body, out_shape=[jax.ShapeDtypeStruct(shape, jnp.float32)...  25 us

profile of v5, /device:TPU:1, one launch (start us, length us, event | category | flops | bytes accessed | tf_op | source)
XLA Modules:
  0.0 127.9 jit_solution(14528743537380170505)
XLA Ops:
  0.6 0.0 copy-start.2
  0.6 0.9 constant_dynamic-update-slice_fusion.1
  1.5 0.0 copy-done.2
  1.5 5.8 %shard_map.83 = f32[16,1,2048]{2,1,0:T(1,128)S(1)} custom-call(bf16[32,2048]{1,0:T(8,128)(2,1)S(1)} %constant_dynamic-update-slice_fusion.xt_ref.refs_0_), custom_call_target="tpu_custom_call" | custom-call | tf_op jit(solution)/shard_map/pallas_call | solution.py:259
  7.3 0.0 copy-start
  7.4 18.1 %all_to_all.35.refs_2_ = f32[16,1,2048]{2,1,0:T(1,128)S(1)} all-to-all(f32[16,1,2048]{2,1,0:T(1,128)S(1)} %shard_map.83), channel_id=1, replica_groups={{8,9,10,11,12,13,14,15,0,1,2,3,4,5,6,7},{24,25,26,27,28,29,30,31,16,17,..., dimensions={0} | all-to-all | bytes 262144 | tf_op jit(solution)/shard_map/all_to_all | solution.py:268
  25.4 0.0 copy-done
  25.4 6.1 %shard_map.84 = (f32[1,2048]{1,0:T(1,128)S(1)}, f32[32,1,2048]{2,1,0:T(1,128)S(1)}) custom-call(bf16[32,2048]{1,0:T(8,128)(2,1)S(1)} %constant_dynamic-update-slice_fusion.xt_ref.refs_0_, f32[1,2048]{1,0:T(1,128)S(1)} %bitcast.5, f32[16,1,2048]{2,1,0:T(1,128)S(1)} %all_to_all.35.refs_2_), custom_call_target="tpu_custom_call" | custom-call | tf_op jit(solution)/shard_map/pallas_call | solution.py:259
  31.6 0.0 copy-start.1
  31.6 17.7 %all_to_all.36.refs_4_ = f32[32,1,2048]{2,1,0:T(1,128)S(1)} all-to-all(f32[32,1,2048]{2,1,0:T(1,128)S(1)} %get-tuple-element.18), channel_id=1, replica_groups={{336,464,80,208,352,480,96,224,368,496,112,240,256,384,0,128,272,400,16..., dimensions={0} | all-to-all | bytes 524288 | tf_op jit(solution)/shard_map/all_to_all | solution.py:268
  49.2 0.0 copy-done.1
  49.2 2.7 %shard_map.85 = (f32[1,2048]{1,0:T(1,128)S(1)}, f32[16,1,2048]{2,1,0:T(1,128)S(1)}) custom-call(bf16[32,2048]{1,0:T(8,128)(2,1)S(1)} %constant_dynamic-update-slice_fusion.xt_ref.refs_0_, f32[1,2048]{1,0:T(1,128)S(1)} %bitcast.6, f32[1,2048]{1,0:T(1,128)S(1)} %bitcast.8, f32[1,2048]{1,0:T(1,128)S(1)} %get-tuple-element.17.refs_3_.refs_2_, ...), custom_call_target="tpu_custom_call" | custom-call | tf_op jit(solution)/shard_map/pallas_call | solution.py:259
  51.9 13.2 %all_to_all.37.refs_4_ = f32[16,1,2048]{2,1,0:T(1,128)S(1)} all-to-all(f32[16,1,2048]{2,1,0:T(1,128)S(1)} %get-tuple-element.20), channel_id=1, replica_groups={{8,9,10,11,12,13,14,15,0,1,2,3,4,5,6,7},{24,25,26,27,28,29,30,31,16,17,..., dimensions={0} | all-to-all | bytes 262144 | tf_op jit(solution)/shard_map/all_to_all | solution.py:268
  65.1 5.2 %shard_map.86 = (f32[1,2048]{1,0:T(1,128)S(1)}, f32[32,1,1152]{2,1,0:T(1,128)S(1)}) custom-call(bf16[32,2048]{1,0:T(8,128)(2,1)S(1)} %constant_dynamic-update-slice_fusion.xt_ref.refs_0_, f32[1,2048]{1,0:T(1,128)S(1)} %bitcast.9, f32[1,2048]{1,0:T(1,128)S(1)} %get-tuple-element.17.refs_3_.refs_2_, f32[1,2048]{1,0:T(1,128)S(1)} %get-tuple-element.19.refs_3_.beta_ref, ...), custom_call_target="tpu_custom_call" | custom-call | tf_op jit(solution)/shard_map/pallas_call | solution.py:259
  70.3 13.4 %all_to_all.38.got_ref = f32[32,1,1152]{2,1,0:T(1,128)S(1)} all-to-all(f32[32,1,1152]{2,1,0:T(1,128)S(1)} %get-tuple-element.22), channel_id=1, replica_groups={{336,464,80,208,352,480,96,224,368,496,112,240,256,384,0,128,272,400,16..., dimensions={0} | all-to-all | bytes 294912 | tf_op jit(solution)/shard_map/all_to_all | solution.py:268
  83.8 0.1 shard_map.87
  83.9 12.7 %all_to_all.39.got_ref = f32[32,1,1152]{2,1,0:T(1,128)S(1)} all-to-all(f32[32,1,1152]{2,1,0:T(1,128)S(1)} %shard_map.87), channel_id=1, replica_groups={{336,464,80,208,352,480,96,224,368,496,112,240,256,384,0,128,272,400,16..., dimensions={0} | all-to-all | bytes 294912 | tf_op jit(solution)/shard_map/all_to_all | solution.py:268
  96.6 4.3 %shard_map.88 = (f32[16,2048]{1,0:T(8,128)}, f32[1,2048]{1,0:T(1,128)}, f32[16,1,2176]{2,1,0:T(1,128)S(1)}) custom-call(bf16[32,2048]{1,0:T(8,128)(2,1)S(1)} %constant_dynamic-update-slice_fusion.xt_ref.refs_0_, f32[1,2048]{1,0:T(1,128)S(1)} %get-tuple-element.21.alpha_ref.refs_2_, f32[1,2048]{1,0:T(1,128)S(1)} %get-tuple-element.19.refs_3_.beta_ref, ...), custom_call_target="tpu_custom_call" | custom-call | tf_op jit(solution)/shard_map/pallas_call | solution.py:259
  100.8 14.5 %all_to_all.40.got_ref = f32[16,1,2176]{2,1,0:T(1,128)S(1)} all-to-all(f32[16,1,2176]{2,1,0:T(1,128)S(1)} %get-tuple-element.23), channel_id=1, replica_groups={{8,9,10,11,12,13,14,15,0,1,2,3,4,5,6,7},{24,25,26,27,28,29,30,31,16,17,..., dimensions={0} | all-to-all | bytes 278528 | tf_op jit(solution)/shard_map/all_to_all | solution.py:268
  115.3 0.1 shard_map.89
  115.4 11.8 %all_to_all.41.refs_3_ = f32[16,1,2176]{2,1,0:T(1,128)S(1)} all-to-all(f32[16,1,2176]{2,1,0:T(1,128)S(1)} %shard_map.89), channel_id=1, replica_groups={{8,9,10,11,12,13,14,15,0,1,2,3,4,5,6,7},{24,25,26,27,28,29,30,31,16,17,..., dimensions={0} | all-to-all | bytes 278528 | tf_op jit(solution)/shard_map/all_to_all | solution.py:268
  127.2 0.7 shard_map.90
  (1 shorter events, 0.0 us)
Async XLA Ops:
  0.6 0.9 copy-start.2
  7.3 18.1 %copy-start = (f32[2048]{0:T(1024)S(1)}, f32[2048]{0:T(1024)}, u32[]{:S(2)}) copy-start(f32[2048]{0:T(1024)} %param.6) | copy-start | bytes 24580
  31.6 17.7 %copy-start.1 = (f32[2048]{0:T(1024)S(1)}, f32[2048]{0:T(1024)}, u32[]{:S(2)}) copy-start(f32[2048]{0:T(1024)} %param.7) | copy-start | bytes 24580

commit v6 on v5

--- a/solution.py
+++ b/solution.py
@@ -17,6 +17,7 @@
 HALF = 8
 INNER = 8
 FIRST = 5
+STRIDE = 3
 SAFE = 2.0**-80
 
 
@@ -279,7 +280,7 @@
     xt = jnp.concatenate([x, t], axis=0)
     outer = n_src // INNER
     by_src = [(r + outer // 2) % outer * INNER + (r // outer + FIRST) % INNER for r in range(n_src)]
-    by_tgt = [(r + n_tgt // 2) % n_tgt for r in range(n_tgt)]
+    by_tgt = [(STRIDE * r + n_tgt // 2) % n_tgt for r in range(n_tgt)]
     assert rows == cols and n_src * LANES == cols * split and n_tgt * LANES == rows
     col_row = (n_src, 1, (HALF + 1) * LANES)
     row_row = (n_tgt, 1, (features + 1) * LANES)

time: 128 us -> 127 us (level)
  blocking collectives: 101 us -> 99.5 us
    all_to_all x7, blocking collectives: 101 us -> 99.5 us  [spread(): lax.all_to_all(parts, axis, 0, 0, axis_index_groups=[order], tiled=True)]
where the time goes in v6:
time: 127 us; the launch traced here: 126 us
  blocking collectives  99.5 us (78%)
  Pallas kernels  25 us (20%)
    all_to_all x7, blocking collectives, spread(): lax.all_to_all(parts, axis, 0, 0, axis_index_groups=[order], tiled=True)  99.5 us
    pallas_call x8, Pallas kernels, call(): pl.pallas_call(body, out_shape=[jax.ShapeDtypeStruct(shape, jnp.float32)...  25 us

profile of v6, /device:TPU:1, one launch (start us, length us, event | category | flops | bytes accessed | tf_op | source)
XLA Modules:
  0.0 126.1 jit_solution(14261628655121130818)
XLA Ops:
  0.6 0.0 copy-start.2
  0.6 0.9 constant_dynamic-update-slice_fusion.1
  1.5 0.0 copy-done.2
  1.5 5.8 %shard_map.83 = f32[16,1,2048]{2,1,0:T(1,128)S(1)} custom-call(bf16[32,2048]{1,0:T(8,128)(2,1)S(1)} %constant_dynamic-update-slice_fusion.xt_ref.refs_0_), custom_call_target="tpu_custom_call" | custom-call | tf_op jit(solution)/shard_map/pallas_call | solution.py:260
  7.3 0.0 copy-start
  7.4 17.7 %all_to_all.35.refs_2_ = f32[16,1,2048]{2,1,0:T(1,128)S(1)} all-to-all(f32[16,1,2048]{2,1,0:T(1,128)S(1)} %shard_map.83), channel_id=1, replica_groups={{8,11,14,1,4,7,10,13,0,3,6,9,12,15,2,5},{24,27,30,17,20,23,26,29,16,19,..., dimensions={0} | all-to-all | bytes 262144 | tf_op jit(solution)/shard_map/all_to_all | solution.py:269
  25.1 0.0 copy-done
  25.1 6.1 %shard_map.84 = (f32[1,2048]{1,0:T(1,128)S(1)}, f32[32,1,2048]{2,1,0:T(1,128)S(1)}) custom-call(bf16[32,2048]{1,0:T(8,128)(2,1)S(1)} %constant_dynamic-update-slice_fusion.xt_ref.refs_0_, f32[1,2048]{1,0:T(1,128)S(1)} %bitcast.5, f32[16,1,2048]{2,1,0:T(1,128)S(1)} %all_to_all.35.refs_2_), custom_call_target="tpu_custom_call" | custom-call | tf_op jit(solution)/shard_map/pallas_call | solution.py:260
  31.3 0.0 copy-start.1
  31.3 18.0 %all_to_all.36.refs_4_ = f32[32,1,2048]{2,1,0:T(1,128)S(1)} all-to-all(f32[32,1,2048]{2,1,0:T(1,128)S(1)} %get-tuple-element.18), channel_id=1, replica_groups={{336,464,80,208,352,480,96,224,368,496,112,240,256,384,0,128,272,400,16..., dimensions={0} | all-to-all | bytes 524288 | tf_op jit(solution)/shard_map/all_to_all | solution.py:269
  49.2 0.0 copy-done.1
  49.2 2.7 %shard_map.85 = (f32[1,2048]{1,0:T(1,128)S(1)}, f32[16,1,2048]{2,1,0:T(1,128)S(1)}) custom-call(bf16[32,2048]{1,0:T(8,128)(2,1)S(1)} %constant_dynamic-update-slice_fusion.xt_ref.refs_0_, f32[1,2048]{1,0:T(1,128)S(1)} %bitcast.6, f32[1,2048]{1,0:T(1,128)S(1)} %bitcast.8, f32[1,2048]{1,0:T(1,128)S(1)} %get-tuple-element.17.refs_3_.refs_2_, ...), custom_call_target="tpu_custom_call" | custom-call | tf_op jit(solution)/shard_map/pallas_call | solution.py:260
  51.9 12.2 %all_to_all.37.refs_4_ = f32[16,1,2048]{2,1,0:T(1,128)S(1)} all-to-all(f32[16,1,2048]{2,1,0:T(1,128)S(1)} %get-tuple-element.20), channel_id=1, replica_groups={{8,11,14,1,4,7,10,13,0,3,6,9,12,15,2,5},{24,27,30,17,20,23,26,29,16,19,..., dimensions={0} | all-to-all | bytes 262144 | tf_op jit(solution)/shard_map/all_to_all | solution.py:269
  64.1 5.2 %shard_map.86 = (f32[1,2048]{1,0:T(1,128)S(1)}, f32[32,1,1152]{2,1,0:T(1,128)S(1)}) custom-call(bf16[32,2048]{1,0:T(8,128)(2,1)S(1)} %constant_dynamic-update-slice_fusion.xt_ref.refs_0_, f32[1,2048]{1,0:T(1,128)S(1)} %bitcast.9, f32[1,2048]{1,0:T(1,128)S(1)} %get-tuple-element.17.refs_3_.refs_2_, f32[1,2048]{1,0:T(1,128)S(1)} %get-tuple-element.19.refs_3_.beta_ref, ...), custom_call_target="tpu_custom_call" | custom-call | tf_op jit(solution)/shard_map/pallas_call | solution.py:260
  69.3 13.6 %all_to_all.38.got_ref = f32[32,1,1152]{2,1,0:T(1,128)S(1)} all-to-all(f32[32,1,1152]{2,1,0:T(1,128)S(1)} %get-tuple-element.22), channel_id=1, replica_groups={{336,464,80,208,352,480,96,224,368,496,112,240,256,384,0,128,272,400,16..., dimensions={0} | all-to-all | bytes 294912 | tf_op jit(solution)/shard_map/all_to_all | solution.py:269
  82.9 0.1 shard_map.87
  83.0 13.2 %all_to_all.39.got_ref = f32[32,1,1152]{2,1,0:T(1,128)S(1)} all-to-all(f32[32,1,1152]{2,1,0:T(1,128)S(1)} %shard_map.87), channel_id=1, replica_groups={{336,464,80,208,352,480,96,224,368,496,112,240,256,384,0,128,272,400,16..., dimensions={0} | all-to-all | bytes 294912 | tf_op jit(solution)/shard_map/all_to_all | solution.py:269
  96.2 4.3 %shard_map.88 = (f32[16,2048]{1,0:T(8,128)}, f32[1,2048]{1,0:T(1,128)}, f32[16,1,2176]{2,1,0:T(1,128)S(1)}) custom-call(bf16[32,2048]{1,0:T(8,128)(2,1)S(1)} %constant_dynamic-update-slice_fusion.xt_ref.refs_0_, f32[1,2048]{1,0:T(1,128)S(1)} %get-tuple-element.21.alpha_ref.refs_2_, f32[1,2048]{1,0:T(1,128)S(1)} %get-tuple-element.19.refs_3_.beta_ref, ...), custom_call_target="tpu_custom_call" | custom-call | tf_op jit(solution)/shard_map/pallas_call | solution.py:260
  100.5 13.1 %all_to_all.40.got_ref = f32[16,1,2176]{2,1,0:T(1,128)S(1)} all-to-all(f32[16,1,2176]{2,1,0:T(1,128)S(1)} %get-tuple-element.23), channel_id=1, replica_groups={{8,11,14,1,4,7,10,13,0,3,6,9,12,15,2,5},{24,27,30,17,20,23,26,29,16,19,..., dimensions={0} | all-to-all | bytes 278528 | tf_op jit(solution)/shard_map/all_to_all | solution.py:269
  113.6 0.1 shard_map.89
  113.6 11.7 %all_to_all.41.refs_3_ = f32[16,1,2176]{2,1,0:T(1,128)S(1)} all-to-all(f32[16,1,2176]{2,1,0:T(1,128)S(1)} %shard_map.89), channel_id=1, replica_groups={{8,11,14,1,4,7,10,13,0,3,6,9,12,15,2,5},{24,27,30,17,20,23,26,29,16,19,..., dimensions={0} | all-to-all | bytes 278528 | tf_op jit(solution)/shard_map/all_to_all | solution.py:269
  125.4 0.7 shard_map.90
  (1 shorter events, 0.0 us)
Async XLA Ops:
  0.6 0.9 copy-start.2
  7.3 17.8 %copy-start = (f32[2048]{0:T(1024)S(1)}, f32[2048]{0:T(1024)}, u32[]{:S(2)}) copy-start(f32[2048]{0:T(1024)} %param.6) | copy-start | bytes 24580
  31.3 18.0 %copy-start.1 = (f32[2048]{0:T(1024)S(1)}, f32[2048]{0:T(1024)}, u32[]{:S(2)}) copy-start(f32[2048]{0:T(1024)} %param.7) | copy-start | bytes 24580

commit v7 on v6

--- a/solution.py
+++ b/solution.py
@@ -105,7 +105,7 @@
         out_ref[d] = total
 
 
-def weighted_columns(a_ref, b_ref, points_ref, out_ref, split, exact):
+def weighted_columns(a_ref, b_ref, points_ref, out_ref, split):
     features = points_ref.shape[0]
     share = features // split
     cols = b_ref.shape[1]
@@ -117,9 +117,6 @@
         points = points_ref[:, at : at + CHUNK]
         rounded = weight.astype(jnp.bfloat16)
         moved = moved + jnp.dot(points, rounded, preferred_element_type=jnp.float32)
-        if exact:
-            rest = (weight - rounded.astype(jnp.float32)).astype(jnp.bfloat16)
-            moved = moved + jnp.dot(points, rest, preferred_element_type=jnp.float32)
     total = jnp.sum(total, axis=0, keepdims=True)
     for q in range(cols // LANES):
         lanes = slice(q * LANES, (q + 1) * LANES)
@@ -203,7 +200,7 @@
     alpha2_ref[...] = alpha
     over = beta_ref[...] - log2_weight(tlogw_ref, whole_t)
     fill_operands(x_ref[...], alpha, t_ref[...], over, a_ref, b_ref)
-    weighted_columns(a_ref, b_ref, x_ref, out_ref, x_ref.shape[0] // HALF, True)
+    weighted_columns(a_ref, b_ref, x_ref, out_ref, x_ref.shape[0] // HALF)
 
 
 def share_means(got_ref, out_ref):
@@ -240,7 +237,7 @@
     beta = beta_ref[...] - jnp.log(mass) * LOG2E
     pot_tgt_ref[...] = beta * (1.0 / KAPPA) + norm_of(t_ref) * (1.0 / t_ref.shape[0])
     fill_operands(t_ref[...], beta, x_ref[...], alpha_ref[...], a_ref, b_ref)
-    weighted_columns(a_ref, b_ref, t_ref, out_ref, 1, False)
+    weighted_columns(a_ref, b_ref, t_ref, out_ref, 1)
 
 
 def finish_rows(whole, xt_ref, logw_ref, alpha_ref, got_ref, projected_ref, ratio_ref, pot_src_ref):

time: 127 us -> 125 us (0.984)
  Pallas kernels: 25 us -> 23.4 us
    pallas_call x8, Pallas kernels: 25 us -> 23.4 us  [call(): pl.pallas_call(body, out_shape=[jax.ShapeDtypeStruct(shape, jnp.float32)...]
where the time goes in v7:
time: 125 us; the launch traced here: 124 us
  blocking collectives  99.5 us (80%)
  Pallas kernels  23.4 us (19%)
    all_to_all x7, blocking collectives, spread(): lax.all_to_all(parts, axis, 0, 0, axis_index_groups=[order], tiled=True)  99.5 us
    pallas_call x8, Pallas kernels, call(): pl.pallas_call(body, out_shape=[jax.ShapeDtypeStruct(shape, jnp.float32)...  23.4 us

profile of v7, /device:TPU:1, one launch (start us, length us, event | category | flops | bytes accessed | tf_op | source)
XLA Modules:
  0.0 124.5 jit_solution(17242899952926824718)
XLA Ops:
  0.6 0.0 copy-start.2
  0.6 0.9 constant_dynamic-update-slice_fusion.1
  1.5 0.0 copy-done.2
  1.5 5.8 %shard_map.83 = f32[16,1,2048]{2,1,0:T(1,128)S(1)} custom-call(bf16[32,2048]{1,0:T(8,128)(2,1)S(1)} %constant_dynamic-update-slice_fusion.xt_ref.refs_0_), custom_call_target="tpu_custom_call" | custom-call | tf_op jit(solution)/shard_map/pallas_call | solution.py:257
  7.3 0.0 copy-start
  7.4 17.7 %all_to_all.35.refs_2_ = f32[16,1,2048]{2,1,0:T(1,128)S(1)} all-to-all(f32[16,1,2048]{2,1,0:T(1,128)S(1)} %shard_map.83), channel_id=1, replica_groups={{8,11,14,1,4,7,10,13,0,3,6,9,12,15,2,5},{24,27,30,17,20,23,26,29,16,19,..., dimensions={0} | all-to-all | bytes 262144 | tf_op jit(solution)/shard_map/all_to_all | solution.py:266
  25.1 0.0 copy-done
  25.1 6.1 %shard_map.84 = (f32[1,2048]{1,0:T(1,128)S(1)}, f32[32,1,2048]{2,1,0:T(1,128)S(1)}) custom-call(bf16[32,2048]{1,0:T(8,128)(2,1)S(1)} %constant_dynamic-update-slice_fusion.xt_ref.refs_0_, f32[1,2048]{1,0:T(1,128)S(1)} %bitcast.5, f32[16,1,2048]{2,1,0:T(1,128)S(1)} %all_to_all.35.refs_2_), custom_call_target="tpu_custom_call" | custom-call | tf_op jit(solution)/shard_map/pallas_call | solution.py:257
  31.3 0.0 copy-start.1
  31.3 18.0 %all_to_all.36.refs_4_ = f32[32,1,2048]{2,1,0:T(1,128)S(1)} all-to-all(f32[32,1,2048]{2,1,0:T(1,128)S(1)} %get-tuple-element.18), channel_id=1, replica_groups={{336,464,80,208,352,480,96,224,368,496,112,240,256,384,0,128,272,400,16..., dimensions={0} | all-to-all | bytes 524288 | tf_op jit(solution)/shard_map/all_to_all | solution.py:266
  49.2 0.0 copy-done.1
  49.2 2.7 %shard_map.85 = (f32[1,2048]{1,0:T(1,128)S(1)}, f32[16,1,2048]{2,1,0:T(1,128)S(1)}) custom-call(bf16[32,2048]{1,0:T(8,128)(2,1)S(1)} %constant_dynamic-update-slice_fusion.xt_ref.refs_0_, f32[1,2048]{1,0:T(1,128)S(1)} %bitcast.6, f32[1,2048]{1,0:T(1,128)S(1)} %bitcast.8, f32[1,2048]{1,0:T(1,128)S(1)} %get-tuple-element.17.refs_3_.refs_2_, ...), custom_call_target="tpu_custom_call" | custom-call | tf_op jit(solution)/shard_map/pallas_call | solution.py:257
  51.9 12.2 %all_to_all.37.refs_4_ = f32[16,1,2048]{2,1,0:T(1,128)S(1)} all-to-all(f32[16,1,2048]{2,1,0:T(1,128)S(1)} %get-tuple-element.20), channel_id=1, replica_groups={{8,11,14,1,4,7,10,13,0,3,6,9,12,15,2,5},{24,27,30,17,20,23,26,29,16,19,..., dimensions={0} | all-to-all | bytes 262144 | tf_op jit(solution)/shard_map/all_to_all | solution.py:266
  64.1 3.7 %shard_map.86 = (f32[1,2048]{1,0:T(1,128)S(1)}, f32[32,1,1152]{2,1,0:T(1,128)S(1)}) custom-call(bf16[32,2048]{1,0:T(8,128)(2,1)S(1)} %constant_dynamic-update-slice_fusion.xt_ref.refs_0_, f32[1,2048]{1,0:T(1,128)S(1)} %bitcast.9, f32[1,2048]{1,0:T(1,128)S(1)} %get-tuple-element.17.refs_3_.refs_2_, f32[1,2048]{1,0:T(1,128)S(1)} %get-tuple-element.19.refs_3_.beta_ref, ...), custom_call_target="tpu_custom_call" | custom-call | tf_op jit(solution)/shard_map/pallas_call | solution.py:257
  67.8 13.6 %all_to_all.38.got_ref = f32[32,1,1152]{2,1,0:T(1,128)S(1)} all-to-all(f32[32,1,1152]{2,1,0:T(1,128)S(1)} %get-tuple-element.22), channel_id=1, replica_groups={{336,464,80,208,352,480,96,224,368,496,112,240,256,384,0,128,272,400,16..., dimensions={0} | all-to-all | bytes 294912 | tf_op jit(solution)/shard_map/all_to_all | solution.py:266
  81.4 0.1 shard_map.87
  81.5 13.2 %all_to_all.39.got_ref = f32[32,1,1152]{2,1,0:T(1,128)S(1)} all-to-all(f32[32,1,1152]{2,1,0:T(1,128)S(1)} %shard_map.87), channel_id=1, replica_groups={{336,464,80,208,352,480,96,224,368,496,112,240,256,384,0,128,272,400,16..., dimensions={0} | all-to-all | bytes 294912 | tf_op jit(solution)/shard_map/all_to_all | solution.py:266
  94.6 4.3 %shard_map.88 = (f32[16,2048]{1,0:T(8,128)}, f32[1,2048]{1,0:T(1,128)}, f32[16,1,2176]{2,1,0:T(1,128)S(1)}) custom-call(bf16[32,2048]{1,0:T(8,128)(2,1)S(1)} %constant_dynamic-update-slice_fusion.xt_ref.refs_0_, f32[1,2048]{1,0:T(1,128)S(1)} %get-tuple-element.21.alpha_ref.refs_2_, f32[1,2048]{1,0:T(1,128)S(1)} %get-tuple-element.19.refs_3_.beta_ref, ...), custom_call_target="tpu_custom_call" | custom-call | tf_op jit(solution)/shard_map/pallas_call | solution.py:257
  98.9 13.1 %all_to_all.40.got_ref = f32[16,1,2176]{2,1,0:T(1,128)S(1)} all-to-all(f32[16,1,2176]{2,1,0:T(1,128)S(1)} %get-tuple-element.23), channel_id=1, replica_groups={{8,11,14,1,4,7,10,13,0,3,6,9,12,15,2,5},{24,27,30,17,20,23,26,29,16,19,..., dimensions={0} | all-to-all | bytes 278528 | tf_op jit(solution)/shard_map/all_to_all | solution.py:266
  112.0 0.1 shard_map.89
  112.1 11.7 %all_to_all.41.refs_3_ = f32[16,1,2176]{2,1,0:T(1,128)S(1)} all-to-all(f32[16,1,2176]{2,1,0:T(1,128)S(1)} %shard_map.89), channel_id=1, replica_groups={{8,11,14,1,4,7,10,13,0,3,6,9,12,15,2,5},{24,27,30,17,20,23,26,29,16,19,..., dimensions={0} | all-to-all | bytes 278528 | tf_op jit(solution)/shard_map/all_to_all | solution.py:266
  123.8 0.7 shard_map.90
  (1 shorter events, 0.0 us)
Async XLA Ops:
  0.6 0.9 copy-start.2
  7.3 17.8 %copy-start = (f32[2048]{0:T(1024)S(1)}, f32[2048]{0:T(1024)}, u32[]{:S(2)}) copy-start(f32[2048]{0:T(1024)} %param.6) | copy-start | bytes 24580
  31.3 18.0 %copy-start.1 = (f32[2048]{0:T(1024)S(1)}, f32[2048]{0:T(1024)}, u32[]{:S(2)}) copy-start(f32[2048]{0:T(1024)} %param.7) | copy-start | bytes 24580

commit v8 on v7

--- a/solution.py
+++ b/solution.py
@@ -56,6 +56,15 @@
     return jnp.dot(a_ref[at : at + count, :], b_ref[...], preferred_element_type=jnp.float32)
 
 
+def pack(row):
+    width = row.shape[1] // 8
+    return jnp.concatenate([row[:, r * width : (r + 1) * width] for r in range(8)], axis=0)
+
+
+def unpack(tile):
+    return jnp.concatenate([tile[r : r + 1, :] for r in range(8)], axis=1)
+
+
 def by_sublane(array):
     return array.reshape(array.shape[0] // 8, 8, array.shape[1])
 
@@ -63,14 +72,14 @@
 def lse_columns(a_ref, b_ref, b_dual, out_ref):
     def store(lse):
         for d in range(out_ref.shape[0]):
-            out_ref[d] = lse - b_dual
-
-    total = total_of(a_ref, b_ref)
+            out_ref[d] = lse - pack(b_dual)
+
+    total = pack(total_of(a_ref, b_ref))
     store(jnp.log(total) * LOG2E)
 
     @pl.when(jnp.min(total) < SAFE)
     def with_peaks():
-        store(lse_of(a_ref, b_ref))
+        store(pack(lse_of(a_ref, b_ref)))
 
 
 def lse_of(a_ref, b_ref):
@@ -100,7 +109,7 @@
 
 
 def sum_columns(a_ref, b_ref, out_ref):
-    total = total_of(a_ref, b_ref)
+    total = pack(total_of(a_ref, b_ref))
     for d in range(out_ref.shape[0]):
         out_ref[d] = total
 
@@ -174,7 +183,7 @@
 
 def first_cols(whole, xt_ref, logw_ref, got_ref, alpha_ref, out_ref, a_ref, b_ref):
     x_ref, t_ref = clouds(xt_ref)
-    alpha = log2_weight(logw_ref, whole) - joined_lse(got_ref)
+    alpha = log2_weight(logw_ref, whole) - unpack(joined_lse(got_ref))
     alpha_ref[...] = alpha
     over = norm_dual(t_ref)
     fill_operands(x_ref[...], alpha, t_ref[...], over, a_ref, b_ref)
@@ -185,7 +194,7 @@
     whole_s, whole_t, xt_ref, slogw_ref, tlogw_ref, alpha_ref, got_ref, beta_ref, out_ref, a_ref, b_ref
 ):
     x_ref, t_ref = clouds(xt_ref)
-    beta = log2_weight(tlogw_ref, whole_t) - joined_lse(got_ref)
+    beta = log2_weight(tlogw_ref, whole_t) - unpack(joined_lse(got_ref))
     beta_ref[...] = beta
     over = alpha_ref[...] - log2_weight(slogw_ref, whole_s)
     fill_operands(t_ref[...], beta, x_ref[...], over, a_ref, b_ref)
@@ -196,7 +205,7 @@
     whole_t, xt_ref, tlogw_ref, alpha_ref, beta_ref, got_ref, alpha2_ref, out_ref, a_ref, b_ref
 ):
     x_ref, t_ref = clouds(xt_ref)
-    alpha = alpha_ref[...] - jnp.log(joined_sum(got_ref)) * LOG2E
+    alpha = alpha_ref[...] - unpack(jnp.log(joined_sum(got_ref)) * LOG2E)
     alpha2_ref[...] = alpha
     over = beta_ref[...] - log2_weight(tlogw_ref, whole_t)
     fill_operands(x_ref[...], alpha, t_ref[...], over, a_ref, b_ref)
@@ -230,18 +239,33 @@
 
 
 def last_rows(
-    xt_ref, alpha_ref, beta_ref, got_ref, pulled_ref, pot_tgt_ref, out_ref, a_ref, b_ref
+    xt_ref, alpha_ref, beta_ref, got_ref, means_ref, beta2_ref, out_ref, a_ref, b_ref
 ):
     x_ref, t_ref = clouds(xt_ref)
-    mass = unpack_means(got_ref, pulled_ref, x_ref.shape[0] // HALF)
+    mass = unpack_means(got_ref, means_ref, x_ref.shape[0] // HALF)
     beta = beta_ref[...] - jnp.log(mass) * LOG2E
-    pot_tgt_ref[...] = beta * (1.0 / KAPPA) + norm_of(t_ref) * (1.0 / t_ref.shape[0])
+    beta2_ref[...] = beta
     fill_operands(t_ref[...], beta, x_ref[...], alpha_ref[...], a_ref, b_ref)
     weighted_columns(a_ref, b_ref, t_ref, out_ref, 1)
 
 
-def finish_rows(whole, xt_ref, logw_ref, alpha_ref, got_ref, projected_ref, ratio_ref, pot_src_ref):
-    x_ref, _ = clouds(xt_ref)
+def finish_rows(
+    whole,
+    xt_ref,
+    logw_ref,
+    alpha_ref,
+    beta_ref,
+    means_ref,
+    got_ref,
+    projected_ref,
+    ratio_ref,
+    pot_src_ref,
+    pulled_ref,
+    pot_tgt_ref,
+):
+    x_ref, t_ref = clouds(xt_ref)
+    pulled_ref[...] = means_ref[...]
+    pot_tgt_ref[...] = beta_ref[...] * (1.0 / KAPPA) + norm_of(t_ref) * (1.0 / t_ref.shape[0])
     mass = unpack_means(got_ref, projected_ref, 1)
     ratio_ref[...] = mass * jnp.exp(math.log(whole) - logw_ref[...]) - 1.0
     pot_src_ref[...] = alpha_ref[...] * (1.0 / KAPPA) + norm_of(x_ref) * (1.0 / x_ref.shape[0])
@@ -283,20 +307,20 @@
     row_row = (n_tgt, 1, (features + 1) * LANES)
     by_row, by_col = (cols, rows), (rows, cols)
 
-    (lse,) = call(first_rows, [(n_tgt, 1, rows)], xt, operands=by_row)
+    (lse,) = call(first_rows, [(n_tgt, 8, rows // 8)], xt, operands=by_row)
     got = spread(lse, "tgt", by_tgt)
 
     def body(*refs):
         first_cols(whole_s, *refs)
 
-    alpha, lse = call(body, [(1, rows), (n_src, 1, cols)], xt, slogw, got, operands=by_col)
+    alpha, lse = call(body, [(1, rows), (n_src, 8, cols // 8)], xt, slogw, got, operands=by_col)
     got = spread(lse, "src", by_src)
 
     def body(*refs):
         second_rows(whole_s, whole_t, *refs)
 
     beta, mass = call(
-        body, [(1, cols), (n_tgt, 1, rows)], xt, slogw, tlogw, alpha, got, operands=by_row
+        body, [(1, cols), (n_tgt, 8, rows // 8)], xt, slogw, tlogw, alpha, got, operands=by_row
     )
     got = spread(mass, "tgt", by_tgt)
 
@@ -309,7 +333,7 @@
     got = spread(sums, "src", by_src)
     (means,) = call(share_means, [col_row], got)
     got = spread(means, "src", by_src)
-    pulled, pot_tgt, sums = call(
+    target_means, beta, sums = call(
         last_rows, [(features, cols), (1, cols), row_row], xt, alpha, beta, got, operands=by_row
     )
     got = spread(sums, "tgt", by_tgt)
@@ -319,8 +343,15 @@
     def body(*refs):
         finish_rows(whole_s, *refs)
 
-    projected, ratio, pot_src = call(
-        body, [(features, rows), (1, rows), (1, rows)], xt, slogw, alpha, got
+    projected, ratio, pot_src, pulled, pot_tgt = call(
+        body,
+        [(features, rows), (1, rows), (1, rows), (features, cols), (1, cols)],
+        xt,
+        slogw,
+        alpha,
+        beta,
+        target_means,
+        got,
     )
     return (pot_src.reshape(rows), pot_tgt.reshape(cols), ratio.reshape(rows), projected, pulled)
 

time: 125 us -> 124 us (level)
  no operation moved by 1% of the time
where the time goes in v8:
time: 124 us
  blocking collectives  99.5 us (80%)
  Pallas kernels  22.6 us (18%)
    all_to_all x7, blocking collectives, spread(): lax.all_to_all(parts, axis, 0, 0, axis_index_groups=[order], tiled=True)  99.5 us
    pallas_call x8, Pallas kernels, call(): pl.pallas_call(body, out_shape=[jax.ShapeDtypeStruct(shape, jnp.float32)...  22.6 us

profile of v8, /device:TPU:1, one launch (start us, length us, event | category | flops | bytes accessed | tf_op | source)
XLA Modules:
  0.0 123.7 jit_solution(16609665842440795356)
XLA Ops:
  0.6 0.0 copy-start.2
  0.6 0.9 constant_dynamic-update-slice_fusion.1
  1.5 0.0 copy-done.2
  1.5 5.8 %shard_map.83 = f32[16,8,256]{2,1,0:T(8,128)S(1)} custom-call(bf16[32,2048]{1,0:T(8,128)(2,1)S(1)} %constant_dynamic-update-slice_fusion.xt_ref.refs_0_), custom_call_target="tpu_custom_call" | custom-call | tf_op jit(solution)/shard_map/pallas_call | solution.py:281
  7.3 0.0 copy-start
  7.4 17.7 %all_to_all.35.refs_2_ = f32[16,8,256]{2,1,0:T(8,128)S(1)} all-to-all(f32[16,8,256]{2,1,0:T(8,128)S(1)} %shard_map.83), channel_id=1, replica_groups={{8,11,14,1,4,7,10,13,0,3,6,9,12,15,2,5},{24,27,30,17,20,23,26,29,16,19,..., dimensions={0} | all-to-all | bytes 262144 | tf_op jit(solution)/shard_map/all_to_all | solution.py:290
  25.1 0.0 copy-done
  25.1 6.0 %shard_map.84 = (f32[1,2048]{1,0:T(1,128)S(1)}, f32[32,8,256]{2,1,0:T(8,128)S(1)}) custom-call(bf16[32,2048]{1,0:T(8,128)(2,1)S(1)} %constant_dynamic-update-slice_fusion.xt_ref.refs_0_, f32[1,2048]{1,0:T(1,128)S(1)} %bitcast.5, f32[16,8,256]{2,1,0:T(8,128)S(1)} %all_to_all.35.refs_2_), custom_call_target="tpu_custom_call" | custom-call | tf_op jit(solution)/shard_map/pallas_call | solution.py:281
  31.2 0.0 copy-start.1
  31.2 18.0 %all_to_all.36.refs_4_ = f32[32,8,256]{2,1,0:T(8,128)S(1)} all-to-all(f32[32,8,256]{2,1,0:T(8,128)S(1)} %get-tuple-element.20), channel_id=1, replica_groups={{336,464,80,208,352,480,96,224,368,496,112,240,256,384,0,128,272,400,16..., dimensions={0} | all-to-all | bytes 524288 | tf_op jit(solution)/shard_map/all_to_all | solution.py:290
  49.1 0.0 copy-done.1
  49.1 2.6 %shard_map.85 = (f32[1,2048]{1,0:T(1,128)S(1)}, f32[16,8,256]{2,1,0:T(8,128)S(1)}) custom-call(bf16[32,2048]{1,0:T(8,128)(2,1)S(1)} %constant_dynamic-update-slice_fusion.xt_ref.refs_0_, f32[1,2048]{1,0:T(1,128)S(1)} %bitcast.6, f32[1,2048]{1,0:T(1,128)S(1)} %bitcast.8, f32[1,2048]{1,0:T(1,128)S(1)} %get-tuple-element.19.refs_3_.refs_2_, ...), custom_call_target="tpu_custom_call" | custom-call | tf_op jit(solution)/shard_map/pallas_call | solution.py:281
  51.7 12.2 %all_to_all.37.refs_4_ = f32[16,8,256]{2,1,0:T(8,128)S(1)} all-to-all(f32[16,8,256]{2,1,0:T(8,128)S(1)} %get-tuple-element.22), channel_id=1, replica_groups={{8,11,14,1,4,7,10,13,0,3,6,9,12,15,2,5},{24,27,30,17,20,23,26,29,16,19,..., dimensions={0} | all-to-all | bytes 262144 | tf_op jit(solution)/shard_map/all_to_all | solution.py:290
  63.9 3.6 %shard_map.86 = (f32[1,2048]{1,0:T(1,128)S(1)}, f32[32,1,1152]{2,1,0:T(1,128)S(1)}) custom-call(bf16[32,2048]{1,0:T(8,128)(2,1)S(1)} %constant_dynamic-update-slice_fusion.xt_ref.refs_0_, f32[1,2048]{1,0:T(1,128)S(1)} %bitcast.9, f32[1,2048]{1,0:T(1,128)S(1)} %get-tuple-element.19.refs_3_.refs_2_, f32[1,2048]{1,0:T(1,128)S(1)} %get-tuple-element.21.refs_3_.beta_ref, ...), custom_call_target="tpu_custom_call" | custom-call | tf_op jit(solution)/shard_map/pallas_call | solution.py:281
  67.5 13.6 %all_to_all.38.got_ref = f32[32,1,1152]{2,1,0:T(1,128)S(1)} all-to-all(f32[32,1,1152]{2,1,0:T(1,128)S(1)} %get-tuple-element.24), channel_id=1, replica_groups={{336,464,80,208,352,480,96,224,368,496,112,240,256,384,0,128,272,400,16..., dimensions={0} | all-to-all | bytes 294912 | tf_op jit(solution)/shard_map/all_to_all | solution.py:290
  81.1 0.1 shard_map.87
  81.2 13.2 %all_to_all.39.got_ref = f32[32,1,1152]{2,1,0:T(1,128)S(1)} all-to-all(f32[32,1,1152]{2,1,0:T(1,128)S(1)} %shard_map.87), channel_id=1, replica_groups={{336,464,80,208,352,480,96,224,368,496,112,240,256,384,0,128,272,400,16..., dimensions={0} | all-to-all | bytes 294912 | tf_op jit(solution)/shard_map/all_to_all | solution.py:290
  94.4 3.7 %shard_map.88 = (f32[16,2048]{1,0:T(8,128)S(1)}, f32[1,2048]{1,0:T(1,128)S(1)}, f32[16,1,2176]{2,1,0:T(1,128)S(1)}) custom-call(bf16[32,2048]{1,0:T(8,128)(2,1)S(1)} %constant_dynamic-update-slice_fusion.xt_ref.refs_0_, f32[1,2048]{1,0:T(1,128)S(1)} %get-tuple-element.23.alpha_ref.refs_2_, f32[1,2048]{1,0:T(1,128)S(1)} %get-tuple-element.21.refs_3_.beta_ref, ...), custom_call_target="tpu_custom_call" | custom-call | tf_op jit(solution)/shard_map/pallas_call | solution.py:281
  98.0 13.1 %all_to_all.40.got_ref = f32[16,1,2176]{2,1,0:T(1,128)S(1)} all-to-all(f32[16,1,2176]{2,1,0:T(1,128)S(1)} %get-tuple-element.27), channel_id=1, replica_groups={{8,11,14,1,4,7,10,13,0,3,6,9,12,15,2,5},{24,27,30,17,20,23,26,29,16,19,..., dimensions={0} | all-to-all | bytes 278528 | tf_op jit(solution)/shard_map/all_to_all | solution.py:290
  111.2 0.1 shard_map.89
  111.3 11.7 %all_to_all.41.refs_5_ = f32[16,1,2176]{2,1,0:T(1,128)S(1)} all-to-all(f32[16,1,2176]{2,1,0:T(1,128)S(1)} %shard_map.89), channel_id=1, replica_groups={{8,11,14,1,4,7,10,13,0,3,6,9,12,15,2,5},{24,27,30,17,20,23,26,29,16,19,..., dimensions={0} | all-to-all | bytes 278528 | tf_op jit(solution)/shard_map/all_to_all | solution.py:290
  123.0 0.7 shard_map.90
  (1 shorter events, 0.0 us)
Async XLA Ops:
  0.6 0.9 copy-start.2
  7.3 17.8 %copy-start = (f32[2048]{0:T(1024)S(1)}, f32[2048]{0:T(1024)}, u32[]{:S(2)}) copy-start(f32[2048]{0:T(1024)} %param.6) | copy-start | bytes 24580
  31.2 18.0 %copy-start.1 = (f32[2048]{0:T(1024)S(1)}, f32[2048]{0:T(1024)}, u32[]{:S(2)}) copy-start(f32[2048]{0:T(1024)} %param.7) | copy-start | bytes 24580

commit v9 on v8

--- a/solution.py
+++ b/solution.py
@@ -11,7 +11,7 @@
 LOG2E = math.log2(math.e)
 KAPPA = LOG2E / EPSILON
 LANES = 128
-CHUNK = 256
+CHUNK = 512
 LSE_CHUNK = 64
 DEPTH = 64
 HALF = 8
@@ -286,8 +286,8 @@
     )(*args)
 
 
-def spread(parts, axis, order):
-    return lax.all_to_all(parts, axis, 0, 0, axis_index_groups=[order], tiled=True)
+def spread(parts, axis, groups):
+    return lax.all_to_all(parts, axis, 0, 0, axis_index_groups=groups, tiled=True)
 
 
 def per_device(x, t, source_logw, target_logw):
@@ -300,8 +300,12 @@
     split = features // HALF
     xt = jnp.concatenate([x, t], axis=0)
     outer = n_src // INNER
-    by_src = [(r + outer // 2) % outer * INNER + (r // outer + FIRST) % INNER for r in range(n_src)]
-    by_tgt = [(STRIDE * r + n_tgt // 2) % n_tgt for r in range(n_tgt)]
+    one_src = [(r + outer // 2) % outer * INNER + (r // outer + FIRST) % INNER for r in range(n_src)]
+    by_src = [
+        [(one_src if t % 2 == 0 else one_src[:1] + one_src[:0:-1])[r] * n_tgt + t for r in range(n_src)]
+        for t in range(n_tgt)
+    ]
+    by_tgt = [[(STRIDE * r + n_tgt // 2) % n_tgt for r in range(n_tgt)]]
     assert rows == cols and n_src * LANES == cols * split and n_tgt * LANES == rows
     col_row = (n_src, 1, (HALF + 1) * LANES)
     row_row = (n_tgt, 1, (features + 1) * LANES)
@@ -314,7 +318,7 @@
         first_cols(whole_s, *refs)
 
     alpha, lse = call(body, [(1, rows), (n_src, 8, cols // 8)], xt, slogw, got, operands=by_col)
-    got = spread(lse, "src", by_src)
+    got = spread(lse, ("src", "tgt"), by_src)
 
     def body(*refs):
         second_rows(whole_s, whole_t, *refs)
@@ -330,9 +334,9 @@
     alpha, sums = call(
         body, [(1, rows), col_row], xt, tlogw, alpha, beta, got, operands=by_col
     )
-    got = spread(sums, "src", by_src)
+    got = spread(sums, ("src", "tgt"), by_src)
     (means,) = call(share_means, [col_row], got)
-    got = spread(means, "src", by_src)
+    got = spread(means, ("src", "tgt"), by_src)
     target_means, beta, sums = call(
         last_rows, [(features, cols), (1, cols), row_row], xt, alpha, beta, got, operands=by_row
     )

time: 124 us -> 124 us (level)
  no operation moved by 1% of the time
where the time goes in v9:
time: 124 us; the launch traced here: 123 us
  blocking collectives  99.4 us (80%)
  Pallas kernels  22.4 us (18%)
    all_to_all x7, blocking collectives, spread(): lax.all_to_all(parts, axis, 0, 0, axis_index_groups=groups, tiled=True)  99.4 us
    pallas_call x8, Pallas kernels, call(): pl.pallas_call(body, out_shape=[jax.ShapeDtypeStruct(shape, jnp.float32)...  22.4 us

profile of v9, /device:TPU:1, one launch (start us, length us, event | category | flops | bytes accessed | tf_op | source)
XLA Modules:
  0.0 123.4 jit_solution(2626557695264300854)
XLA Ops:
  0.6 0.0 copy-start.2
  0.6 0.9 constant_dynamic-update-slice_fusion.1
  1.5 0.0 copy-done.2
  1.5 5.8 %shard_map.83 = f32[16,8,256]{2,1,0:T(8,128)S(1)} custom-call(bf16[32,2048]{1,0:T(8,128)(2,1)S(1)} %constant_dynamic-update-slice_fusion.xt_ref.refs_0_), custom_call_target="tpu_custom_call" | custom-call | tf_op jit(solution)/shard_map/pallas_call | solution.py:281
  7.3 0.0 copy-start
  7.3 17.8 %all_to_all.35.refs_2_ = f32[16,8,256]{2,1,0:T(8,128)S(1)} all-to-all(f32[16,8,256]{2,1,0:T(8,128)S(1)} %shard_map.83), channel_id=1, replica_groups={{8,11,14,1,4,7,10,13,0,3,6,9,12,15,2,5},{24,27,30,17,20,23,26,29,16,19,..., dimensions={0} | all-to-all | bytes 262144 | tf_op jit(solution)/shard_map/all_to_all | solution.py:290
  25.1 0.0 copy-done
  25.1 6.0 %shard_map.84 = (f32[1,2048]{1,0:T(1,128)S(1)}, f32[32,8,256]{2,1,0:T(8,128)S(1)}) custom-call(bf16[32,2048]{1,0:T(8,128)(2,1)S(1)} %constant_dynamic-update-slice_fusion.xt_ref.refs_0_, f32[1,2048]{1,0:T(1,128)S(1)} %bitcast.5, f32[16,8,256]{2,1,0:T(8,128)S(1)} %all_to_all.35.refs_2_), custom_call_target="tpu_custom_call" | custom-call | tf_op jit(solution)/shard_map/pallas_call | solution.py:281
  31.1 0.0 copy-start.1
  31.1 18.0 %all_to_all.36.refs_4_ = f32[32,8,256]{2,1,0:T(8,128)S(1)} all-to-all(f32[32,8,256]{2,1,0:T(8,128)S(1)} %get-tuple-element.20), channel_id=1, replica_groups={{336,464,80,208,352,480,96,224,368,496,112,240,256,384,0,128,272,400,16..., dimensions={0} | all-to-all | bytes 524288 | tf_op jit(solution)/shard_map/all_to_all | solution.py:290
  49.2 0.0 copy-done.1
  49.2 2.6 %shard_map.85 = (f32[1,2048]{1,0:T(1,128)S(1)}, f32[16,8,256]{2,1,0:T(8,128)S(1)}) custom-call(bf16[32,2048]{1,0:T(8,128)(2,1)S(1)} %constant_dynamic-update-slice_fusion.xt_ref.refs_0_, f32[1,2048]{1,0:T(1,128)S(1)} %bitcast.6, f32[1,2048]{1,0:T(1,128)S(1)} %bitcast.8, f32[1,2048]{1,0:T(1,128)S(1)} %get-tuple-element.19.refs_3_.refs_2_, ...), custom_call_target="tpu_custom_call" | custom-call | tf_op jit(solution)/shard_map/pallas_call | solution.py:281
  51.8 12.2 %all_to_all.37.refs_4_ = f32[16,8,256]{2,1,0:T(8,128)S(1)} all-to-all(f32[16,8,256]{2,1,0:T(8,128)S(1)} %get-tuple-element.22), channel_id=1, replica_groups={{8,11,14,1,4,7,10,13,0,3,6,9,12,15,2,5},{24,27,30,17,20,23,26,29,16,19,..., dimensions={0} | all-to-all | bytes 262144 | tf_op jit(solution)/shard_map/all_to_all | solution.py:290
  64.0 3.6 %shard_map.86 = (f32[1,2048]{1,0:T(1,128)S(1)}, f32[32,1,1152]{2,1,0:T(1,128)S(1)}) custom-call(bf16[32,2048]{1,0:T(8,128)(2,1)S(1)} %constant_dynamic-update-slice_fusion.xt_ref.refs_0_, f32[1,2048]{1,0:T(1,128)S(1)} %bitcast.9, f32[1,2048]{1,0:T(1,128)S(1)} %get-tuple-element.19.refs_3_.refs_2_, f32[1,2048]{1,0:T(1,128)S(1)} %get-tuple-element.21.refs_3_.beta_ref, ...), custom_call_target="tpu_custom_call" | custom-call | tf_op jit(solution)/shard_map/pallas_call | solution.py:281
  67.6 13.3 %all_to_all.38.got_ref = f32[32,1,1152]{2,1,0:T(1,128)S(1)} all-to-all(f32[32,1,1152]{2,1,0:T(1,128)S(1)} %get-tuple-element.24), channel_id=1, replica_groups={{336,464,80,208,352,480,96,224,368,496,112,240,256,384,0,128,272,400,16..., dimensions={0} | all-to-all | bytes 294912 | tf_op jit(solution)/shard_map/all_to_all | solution.py:290
  80.9 0.1 shard_map.87
  81.0 13.2 %all_to_all.39.got_ref = f32[32,1,1152]{2,1,0:T(1,128)S(1)} all-to-all(f32[32,1,1152]{2,1,0:T(1,128)S(1)} %shard_map.87), channel_id=1, replica_groups={{336,464,80,208,352,480,96,224,368,496,112,240,256,384,0,128,272,400,16..., dimensions={0} | all-to-all | bytes 294912 | tf_op jit(solution)/shard_map/all_to_all | solution.py:290
  94.2 3.5 %shard_map.88 = (f32[16,2048]{1,0:T(8,128)S(1)}, f32[1,2048]{1,0:T(1,128)S(1)}, f32[16,1,2176]{2,1,0:T(1,128)S(1)}) custom-call(bf16[32,2048]{1,0:T(8,128)(2,1)S(1)} %constant_dynamic-update-slice_fusion.xt_ref.refs_0_, f32[1,2048]{1,0:T(1,128)S(1)} %get-tuple-element.23.alpha_ref.refs_2_, f32[1,2048]{1,0:T(1,128)S(1)} %get-tuple-element.21.refs_3_.beta_ref, ...), custom_call_target="tpu_custom_call" | custom-call | tf_op jit(solution)/shard_map/pallas_call | solution.py:281
  97.7 13.1 %all_to_all.40.got_ref = f32[16,1,2176]{2,1,0:T(1,128)S(1)} all-to-all(f32[16,1,2176]{2,1,0:T(1,128)S(1)} %get-tuple-element.27), channel_id=1, replica_groups={{8,11,14,1,4,7,10,13,0,3,6,9,12,15,2,5},{24,27,30,17,20,23,26,29,16,19,..., dimensions={0} | all-to-all | bytes 278528 | tf_op jit(solution)/shard_map/all_to_all | solution.py:290
  110.8 0.1 shard_map.89
  110.9 11.7 %all_to_all.41.refs_5_ = f32[16,1,2176]{2,1,0:T(1,128)S(1)} all-to-all(f32[16,1,2176]{2,1,0:T(1,128)S(1)} %shard_map.89), channel_id=1, replica_groups={{8,11,14,1,4,7,10,13,0,3,6,9,12,15,2,5},{24,27,30,17,20,23,26,29,16,19,..., dimensions={0} | all-to-all | bytes 278528 | tf_op jit(solution)/shard_map/all_to_all | solution.py:290
  122.7 0.7 shard_map.90
  (1 shorter events, 0.0 us)
Async XLA Ops:
  0.6 0.9 copy-start.2
  7.3 17.8 %copy-start = (f32[2048]{0:T(1024)S(1)}, f32[2048]{0:T(1024)}, u32[]{:S(2)}) copy-start(f32[2048]{0:T(1024)} %param.6) | copy-start | bytes 24580
  31.1 18.1 %copy-start.1 = (f32[2048]{0:T(1024)S(1)}, f32[2048]{0:T(1024)}, u32[]{:S(2)}) copy-start(f32[2048]{0:T(1024)} %param.7) | copy-start | bytes 24580

commit v10 on v8

--- a/solution.py
+++ b/solution.py
@@ -13,10 +13,11 @@
 LANES = 128
 CHUNK = 256
 LSE_CHUNK = 64
+WEIGHTED_CHUNK = 512
 DEPTH = 64
 HALF = 8
 INNER = 8
-FIRST = 5
+FIRST = 4
 STRIDE = 3
 SAFE = 2.0**-80
 
@@ -120,10 +121,10 @@
     cols = b_ref.shape[1]
     total = jnp.zeros((8, cols), jnp.float32)
     moved = jnp.zeros((features, cols), jnp.float32)
-    for at in range(0, a_ref.shape[0], CHUNK):
-        weight = jnp.exp2(score_chunk(a_ref, b_ref, at, CHUNK))
+    for at in range(0, a_ref.shape[0], WEIGHTED_CHUNK):
+        weight = jnp.exp2(score_chunk(a_ref, b_ref, at, WEIGHTED_CHUNK))
         total = total + jnp.sum(by_sublane(weight), axis=0)
-        points = points_ref[:, at : at + CHUNK]
+        points = points_ref[:, at : at + WEIGHTED_CHUNK]
         rounded = weight.astype(jnp.bfloat16)
         moved = moved + jnp.dot(points, rounded, preferred_element_type=jnp.float32)
     total = jnp.sum(total, axis=0, keepdims=True)

time: 124 us -> 124 us (level)
  no operation moved by 1% of the time
where the time goes in v10:
time: 124 us
  blocking collectives  99.6 us (80%)
  Pallas kernels  22.4 us (18%)
    all_to_all x7, blocking collectives, spread(): lax.all_to_all(parts, axis, 0, 0, axis_index_groups=[order], tiled=True)  99.6 us
    pallas_call x8, Pallas kernels, call(): pl.pallas_call(body, out_shape=[jax.ShapeDtypeStruct(shape, jnp.float32)...  22.4 us

profile of v10, /device:TPU:1, one launch (start us, length us, event | category | flops | bytes accessed | tf_op | source)
XLA Modules:
  0.0 123.7 jit_solution(13920434859641109580)
XLA Ops:
  0.6 0.0 copy-start.2
  0.6 0.9 constant_dynamic-update-slice_fusion.1
  1.5 0.0 copy-done.2
  1.5 5.8 %shard_map.83 = f32[16,8,256]{2,1,0:T(8,128)S(1)} custom-call(bf16[32,2048]{1,0:T(8,128)(2,1)S(1)} %constant_dynamic-update-slice_fusion.xt_ref.refs_0_), custom_call_target="tpu_custom_call" | custom-call | tf_op jit(solution)/shard_map/pallas_call | solution.py:282
  7.3 0.0 copy-start
  7.4 17.7 %all_to_all.35.refs_2_ = f32[16,8,256]{2,1,0:T(8,128)S(1)} all-to-all(f32[16,8,256]{2,1,0:T(8,128)S(1)} %shard_map.83), channel_id=1, replica_groups={{8,11,14,1,4,7,10,13,0,3,6,9,12,15,2,5},{24,27,30,17,20,23,26,29,16,19,..., dimensions={0} | all-to-all | bytes 262144 | tf_op jit(solution)/shard_map/all_to_all | solution.py:291
  25.1 0.0 copy-done
  25.1 6.0 %shard_map.84 = (f32[1,2048]{1,0:T(1,128)S(1)}, f32[32,8,256]{2,1,0:T(8,128)S(1)}) custom-call(bf16[32,2048]{1,0:T(8,128)(2,1)S(1)} %constant_dynamic-update-slice_fusion.xt_ref.refs_0_, f32[1,2048]{1,0:T(1,128)S(1)} %bitcast.5, f32[16,8,256]{2,1,0:T(8,128)S(1)} %all_to_all.35.refs_2_), custom_call_target="tpu_custom_call" | custom-call | tf_op jit(solution)/shard_map/pallas_call | solution.py:282
  31.2 0.0 copy-start.1
  31.2 18.6 %all_to_all.36.refs_4_ = f32[32,8,256]{2,1,0:T(8,128)S(1)} all-to-all(f32[32,8,256]{2,1,0:T(8,128)S(1)} %get-tuple-element.20), channel_id=1, replica_groups={{320,448,64,192,336,464,80,208,352,480,96,224,368,496,112,240,256,384,0..., dimensions={0} | all-to-all | bytes 524288 | tf_op jit(solution)/shard_map/all_to_all | solution.py:291
  49.7 0.0 copy-done.1
  49.7 2.6 %shard_map.85 = (f32[1,2048]{1,0:T(1,128)S(1)}, f32[16,8,256]{2,1,0:T(8,128)S(1)}) custom-call(bf16[32,2048]{1,0:T(8,128)(2,1)S(1)} %constant_dynamic-update-slice_fusion.xt_ref.refs_0_, f32[1,2048]{1,0:T(1,128)S(1)} %bitcast.6, f32[1,2048]{1,0:T(1,128)S(1)} %bitcast.8, f32[1,2048]{1,0:T(1,128)S(1)} %get-tuple-element.19.refs_3_.refs_2_, ...), custom_call_target="tpu_custom_call" | custom-call | tf_op jit(solution)/shard_map/pallas_call | solution.py:282
  52.3 11.7 %all_to_all.37.refs_4_ = f32[16,8,256]{2,1,0:T(8,128)S(1)} all-to-all(f32[16,8,256]{2,1,0:T(8,128)S(1)} %get-tuple-element.22), channel_id=1, replica_groups={{8,11,14,1,4,7,10,13,0,3,6,9,12,15,2,5},{24,27,30,17,20,23,26,29,16,19,..., dimensions={0} | all-to-all | bytes 262144 | tf_op jit(solution)/shard_map/all_to_all | solution.py:291
  64.0 3.6 %shard_map.86 = (f32[1,2048]{1,0:T(1,128)S(1)}, f32[32,1,1152]{2,1,0:T(1,128)S(1)}) custom-call(bf16[32,2048]{1,0:T(8,128)(2,1)S(1)} %constant_dynamic-update-slice_fusion.xt_ref.refs_0_, f32[1,2048]{1,0:T(1,128)S(1)} %bitcast.9, f32[1,2048]{1,0:T(1,128)S(1)} %get-tuple-element.19.refs_3_.refs_2_, f32[1,2048]{1,0:T(1,128)S(1)} %get-tuple-element.21.refs_3_.beta_ref, ...), custom_call_target="tpu_custom_call" | custom-call | tf_op jit(solution)/shard_map/pallas_call | solution.py:282
  67.6 14.1 %all_to_all.38.got_ref = f32[32,1,1152]{2,1,0:T(1,128)S(1)} all-to-all(f32[32,1,1152]{2,1,0:T(1,128)S(1)} %get-tuple-element.24), channel_id=1, replica_groups={{320,448,64,192,336,464,80,208,352,480,96,224,368,496,112,240,256,384,0..., dimensions={0} | all-to-all | bytes 294912 | tf_op jit(solution)/shard_map/all_to_all | solution.py:291
  81.7 0.1 shard_map.87
  81.8 12.3 %all_to_all.39.got_ref = f32[32,1,1152]{2,1,0:T(1,128)S(1)} all-to-all(f32[32,1,1152]{2,1,0:T(1,128)S(1)} %shard_map.87), channel_id=1, replica_groups={{320,448,64,192,336,464,80,208,352,480,96,224,368,496,112,240,256,384,0..., dimensions={0} | all-to-all | bytes 294912 | tf_op jit(solution)/shard_map/all_to_all | solution.py:291
  94.2 3.5 %shard_map.88 = (f32[16,2048]{1,0:T(8,128)S(1)}, f32[1,2048]{1,0:T(1,128)S(1)}, f32[16,1,2176]{2,1,0:T(1,128)S(1)}) custom-call(bf16[32,2048]{1,0:T(8,128)(2,1)S(1)} %constant_dynamic-update-slice_fusion.xt_ref.refs_0_, f32[1,2048]{1,0:T(1,128)S(1)} %get-tuple-element.23.alpha_ref.refs_2_, f32[1,2048]{1,0:T(1,128)S(1)} %get-tuple-element.21.refs_3_.beta_ref, ...), custom_call_target="tpu_custom_call" | custom-call | tf_op jit(solution)/shard_map/pallas_call | solution.py:282
  97.7 13.4 %all_to_all.40.got_ref = f32[16,1,2176]{2,1,0:T(1,128)S(1)} all-to-all(f32[16,1,2176]{2,1,0:T(1,128)S(1)} %get-tuple-element.27), channel_id=1, replica_groups={{8,11,14,1,4,7,10,13,0,3,6,9,12,15,2,5},{24,27,30,17,20,23,26,29,16,19,..., dimensions={0} | all-to-all | bytes 278528 | tf_op jit(solution)/shard_map/all_to_all | solution.py:291
  111.1 0.1 shard_map.89
  111.2 11.7 %all_to_all.41.refs_5_ = f32[16,1,2176]{2,1,0:T(1,128)S(1)} all-to-all(f32[16,1,2176]{2,1,0:T(1,128)S(1)} %shard_map.89), channel_id=1, replica_groups={{8,11,14,1,4,7,10,13,0,3,6,9,12,15,2,5},{24,27,30,17,20,23,26,29,16,19,..., dimensions={0} | all-to-all | bytes 278528 | tf_op jit(solution)/shard_map/all_to_all | solution.py:291
  123.0 0.7 shard_map.90
  (1 shorter events, 0.0 us)
Async XLA Ops:
  0.6 0.9 copy-start.2
  7.3 17.8 %copy-start = (f32[2048]{0:T(1024)S(1)}, f32[2048]{0:T(1024)}, u32[]{:S(2)}) copy-start(f32[2048]{0:T(1024)} %param.6) | copy-start | bytes 24580
  31.2 18.6 %copy-start.1 = (f32[2048]{0:T(1024)S(1)}, f32[2048]{0:T(1024)}, u32[]{:S(2)}) copy-start(f32[2048]{0:T(1024)} %param.7) | copy-start | bytes 24580

commit v11 on v8

--- a/solution.py
+++ b/solution.py
@@ -17,7 +17,7 @@
 HALF = 8
 INNER = 8
 FIRST = 5
-STRIDE = 3
+STRIDE = 11
 SAFE = 2.0**-80
 
 

time: 124 us -> 125 us (level)
  no operation moved by 1% of the time
where the time goes in v11:
time: 125 us
  blocking collectives  100 us (80%)
  Pallas kernels  22.6 us (18%)
    all_to_all x7, blocking collectives, spread(): lax.all_to_all(parts, axis, 0, 0, axis_index_groups=[order], tiled=True)  100 us
    pallas_call x8, Pallas kernels, call(): pl.pallas_call(body, out_shape=[jax.ShapeDtypeStruct(shape, jnp.float32)...  22.6 us

profile of v11, /device:TPU:1, one launch (start us, length us, event | category | flops | bytes accessed | tf_op | source)
XLA Modules:
  0.0 124.6 jit_solution(9576856911611146053)
XLA Ops:
  0.6 0.0 copy-start.2
  0.6 0.9 constant_dynamic-update-slice_fusion.1
  1.5 0.0 copy-done.2
  1.5 5.8 %shard_map.83 = f32[16,8,256]{2,1,0:T(8,128)S(1)} custom-call(bf16[32,2048]{1,0:T(8,128)(2,1)S(1)} %constant_dynamic-update-slice_fusion.xt_ref.refs_0_), custom_call_target="tpu_custom_call" | custom-call | tf_op jit(solution)/shard_map/pallas_call | solution.py:281
  7.3 0.0 copy-start
  7.4 17.7 %all_to_all.35.refs_2_ = f32[16,8,256]{2,1,0:T(8,128)S(1)} all-to-all(f32[16,8,256]{2,1,0:T(8,128)S(1)} %shard_map.83), channel_id=1, replica_groups={{8,3,14,9,4,15,10,5,0,11,6,1,12,7,2,13},{24,19,30,25,20,31,26,21,16,27,..., dimensions={0} | all-to-all | bytes 262144 | tf_op jit(solution)/shard_map/all_to_all | solution.py:290
  25.1 0.0 copy-done
  25.1 6.0 %shard_map.84 = (f32[1,2048]{1,0:T(1,128)S(1)}, f32[32,8,256]{2,1,0:T(8,128)S(1)}) custom-call(bf16[32,2048]{1,0:T(8,128)(2,1)S(1)} %constant_dynamic-update-slice_fusion.xt_ref.refs_0_, f32[1,2048]{1,0:T(1,128)S(1)} %bitcast.5, f32[16,8,256]{2,1,0:T(8,128)S(1)} %all_to_all.35.refs_2_), custom_call_target="tpu_custom_call" | custom-call | tf_op jit(solution)/shard_map/pallas_call | solution.py:281
  31.1 0.0 copy-start.1
  31.2 17.8 %all_to_all.36.refs_4_ = f32[32,8,256]{2,1,0:T(8,128)S(1)} all-to-all(f32[32,8,256]{2,1,0:T(8,128)S(1)} %get-tuple-element.20), channel_id=1, replica_groups={{336,464,80,208,352,480,96,224,368,496,112,240,256,384,0,128,272,400,16..., dimensions={0} | all-to-all | bytes 524288 | tf_op jit(solution)/shard_map/all_to_all | solution.py:290
  48.9 0.0 copy-done.1
  48.9 2.6 %shard_map.85 = (f32[1,2048]{1,0:T(1,128)S(1)}, f32[16,8,256]{2,1,0:T(8,128)S(1)}) custom-call(bf16[32,2048]{1,0:T(8,128)(2,1)S(1)} %constant_dynamic-update-slice_fusion.xt_ref.refs_0_, f32[1,2048]{1,0:T(1,128)S(1)} %bitcast.6, f32[1,2048]{1,0:T(1,128)S(1)} %bitcast.8, f32[1,2048]{1,0:T(1,128)S(1)} %get-tuple-element.19.refs_3_.refs_2_, ...), custom_call_target="tpu_custom_call" | custom-call | tf_op jit(solution)/shard_map/pallas_call | solution.py:281
  51.5 12.8 %all_to_all.37.refs_4_ = f32[16,8,256]{2,1,0:T(8,128)S(1)} all-to-all(f32[16,8,256]{2,1,0:T(8,128)S(1)} %get-tuple-element.22), channel_id=1, replica_groups={{8,3,14,9,4,15,10,5,0,11,6,1,12,7,2,13},{24,19,30,25,20,31,26,21,16,27,..., dimensions={0} | all-to-all | bytes 262144 | tf_op jit(solution)/shard_map/all_to_all | solution.py:290
  64.3 3.6 %shard_map.86 = (f32[1,2048]{1,0:T(1,128)S(1)}, f32[32,1,1152]{2,1,0:T(1,128)S(1)}) custom-call(bf16[32,2048]{1,0:T(8,128)(2,1)S(1)} %constant_dynamic-update-slice_fusion.xt_ref.refs_0_, f32[1,2048]{1,0:T(1,128)S(1)} %bitcast.9, f32[1,2048]{1,0:T(1,128)S(1)} %get-tuple-element.19.refs_3_.refs_2_, f32[1,2048]{1,0:T(1,128)S(1)} %get-tuple-element.21.refs_3_.beta_ref, ...), custom_call_target="tpu_custom_call" | custom-call | tf_op jit(solution)/shard_map/pallas_call | solution.py:281
  68.0 13.3 %all_to_all.38.got_ref = f32[32,1,1152]{2,1,0:T(1,128)S(1)} all-to-all(f32[32,1,1152]{2,1,0:T(1,128)S(1)} %get-tuple-element.24), channel_id=1, replica_groups={{336,464,80,208,352,480,96,224,368,496,112,240,256,384,0,128,272,400,16..., dimensions={0} | all-to-all | bytes 294912 | tf_op jit(solution)/shard_map/all_to_all | solution.py:290
  81.3 0.1 shard_map.87
  81.4 12.9 %all_to_all.39.got_ref = f32[32,1,1152]{2,1,0:T(1,128)S(1)} all-to-all(f32[32,1,1152]{2,1,0:T(1,128)S(1)} %shard_map.87), channel_id=1, replica_groups={{336,464,80,208,352,480,96,224,368,496,112,240,256,384,0,128,272,400,16..., dimensions={0} | all-to-all | bytes 294912 | tf_op jit(solution)/shard_map/all_to_all | solution.py:290
  94.3 3.7 %shard_map.88 = (f32[16,2048]{1,0:T(8,128)S(1)}, f32[1,2048]{1,0:T(1,128)S(1)}, f32[16,1,2176]{2,1,0:T(1,128)S(1)}) custom-call(bf16[32,2048]{1,0:T(8,128)(2,1)S(1)} %constant_dynamic-update-slice_fusion.xt_ref.refs_0_, f32[1,2048]{1,0:T(1,128)S(1)} %get-tuple-element.23.alpha_ref.refs_2_, f32[1,2048]{1,0:T(1,128)S(1)} %get-tuple-element.21.refs_3_.beta_ref, ...), custom_call_target="tpu_custom_call" | custom-call | tf_op jit(solution)/shard_map/pallas_call | solution.py:281
  98.0 14.0 %all_to_all.40.got_ref = f32[16,1,2176]{2,1,0:T(1,128)S(1)} all-to-all(f32[16,1,2176]{2,1,0:T(1,128)S(1)} %get-tuple-element.27), channel_id=1, replica_groups={{8,3,14,9,4,15,10,5,0,11,6,1,12,7,2,13},{24,19,30,25,20,31,26,21,16,27,..., dimensions={0} | all-to-all | bytes 278528 | tf_op jit(solution)/shard_map/all_to_all | solution.py:290
  112.0 0.1 shard_map.89
  112.1 11.8 %all_to_all.41.refs_5_ = f32[16,1,2176]{2,1,0:T(1,128)S(1)} all-to-all(f32[16,1,2176]{2,1,0:T(1,128)S(1)} %shard_map.89), channel_id=1, replica_groups={{8,3,14,9,4,15,10,5,0,11,6,1,12,7,2,13},{24,19,30,25,20,31,26,21,16,27,..., dimensions={0} | all-to-all | bytes 278528 | tf_op jit(solution)/shard_map/all_to_all | solution.py:290
  123.9 0.7 shard_map.90
  (1 shorter events, 0.0 us)
Async XLA Ops:
  0.6 0.9 copy-start.2
  7.3 17.8 %copy-start = (f32[2048]{0:T(1024)S(1)}, f32[2048]{0:T(1024)}, u32[]{:S(2)}) copy-start(f32[2048]{0:T(1024)} %param.6) | copy-start | bytes 24580
  31.1 17.8 %copy-start.1 = (f32[2048]{0:T(1024)S(1)}, f32[2048]{0:T(1024)}, u32[]{:S(2)}) copy-start(f32[2048]{0:T(1024)} %param.7) | copy-start | bytes 24580
